TPU v7x, 32 devices: a whole 2x2x4 slice. The times are simulated.
32 devices in a mesh: dp: 4 (over y, x), row: 4 (over z), col: 2 (over core).
Axes of the slice: x: 2, y: 2, z: 4, core: 2. Of those that a mesh axis runs over, the one named last changes fastest.
Arguments:
- tokens: bfloat16 [4096, 896], P(('dp', 'row')), may hold values from -6 to 6
- segment_ids: int32 [4096], P(('dp', 'row')), may hold values from 0 to 2, as said below
- attn_gain: bfloat16 [896], replicated, may hold values from 0.099609375 to 1.8984375
- w_query: bfloat16 [896, 896], P('row', 'col'), may hold values from -0.1875 to 0.1875
- b_query: bfloat16 [896], P('col'), may hold values from -3 to 3
- w_key: bfloat16 [896, 128], P('row', 'col'), may hold values from -0.1875 to 0.1875
- b_key: bfloat16 [128], P('col'), may hold values from -3 to 3
- w_value: bfloat16 [896, 128], P('row', 'col'), may hold values from -0.1875 to 0.1875
- b_value: bfloat16 [128], P('col'), may hold values from -0.59765625 to 0.59765625
- w_out: bfloat16 [896, 896], P('col', 'row'), may hold values from -1 to 1
- ffn_gain: bfloat16 [896], replicated, may hold values from 0.099609375 to 1.8984375
- w_gate: bfloat16 [896, 4864], P('row', 'col'), may hold values from -0.1875 to 0.1875
- w_up: bfloat16 [896, 4864], P('row', 'col'), may hold values from -0.1875 to 0.1875
- w_down: bfloat16 [4864, 896], P('col', 'row'), may hold values from -0.078125 to 0.078125
- out_grad: bfloat16 [4096, 896], P(('dp', 'row')), may hold values from -8 to 8
Outputs:
- output: bfloat16 [4096, 896], P(('dp', 'row'))
- grad_tokens: bfloat16 [4096, 896], P(('dp', 'row'))
- grad_attn_gain: float32 [896], replicated
- grad_w_query: float32 [896, 896], P('row', 'col')
- grad_b_query: float32 [896], P('col')
- grad_w_key: float32 [896, 128], P('row', 'col')
- grad_b_key: float32 [128], P('col')
- grad_w_value: float32 [896, 128], P('row', 'col')
- grad_b_value: float32 [128], P('col')
- grad_w_out: float32 [896, 896], P('col', 'row')
- grad_ffn_gain: float32 [896], replicated
- grad_w_gate: float32 [896, 4864], P('row', 'col')
- grad_w_up: float32 [896, 4864], P('row', 'col')
- grad_w_down: float32 [4864, 896], P('col', 'row')
Inputs may be any that keep to these rules, and one draw needn't show every extreme that they name: `segment_ids`: within each sequence of 1024 tokens the ids never fall; id 1 is one document that begins among the first 256 tokens and ends among the last 256; id 0 covers the tokens before it and id 2 those after it.
All inputs are finite; a program needn't handle non-finite values.
Results may differ from a plain program's by a relative error of at most 0.035.
Values may be sent and summed in bfloat16 or wider, within the bound.
No kernel may reach another device: no remote copies, remote signals or barrier semaphores. Data moves between devices by JAX's collectives and lax.ppermute only.
A program may use at most 128 MiB of HBM per device.

v0:
```python
import jax
import jax.numpy as jnp
from jax import lax
from jax.sharding import PartitionSpec as P

HD = 64


NORM_EPS = 1e-06
ROPE_BASE = 1000000.0
NEG_BIG = -1e30
CONTRACT_ROWS = (((0,), (0,)), ((), ()))
CONTRACT_COLS = (((1,), (1,)), ((), ()))


def shortened(array):

    def short(part):
        return part.astype(jnp.bfloat16) if part.dtype == jnp.float32 else part

    return jax.tree.map(short, array)


def rope_tables(positions, head_size):
    ladder = jnp.arange(head_size // 2, dtype=jnp.float32) * (2.0 / head_size)
    frequency = jnp.exp(-ladder * jnp.log(ROPE_BASE))
    angles = positions[:, None] * frequency[None, :]
    return (jnp.cos(angles), jnp.sin(angles))


def rotate(values, cos_table, sin_table):
    half_size = values.shape[-1] // 2
    lower = values[..., :half_size]
    upper = values[..., half_size:]
    cos_part = cos_table[:, None, :]
    sin_part = sin_table[:, None, :]
    return jnp.concatenate(
        [lower * cos_part - upper * sin_part, upper * cos_part + lower * sin_part], axis=-1
    )


def norm_rows(values, gain):
    inv_rms = lax.rsqrt(jnp.mean(values * values, axis=1, keepdims=True) + NORM_EPS)
    unit_rows = values * inv_rms
    return (unit_rows, inv_rms, unit_rows * gain[None, :])


def norm_back(gradient, unit_rows, inv_rms, gain):
    scaled = gradient * gain[None, :]
    inner = jnp.mean(scaled * unit_rows, axis=1, keepdims=True)
    return (inv_rms * (scaled - unit_rows * inner), jnp.sum(gradient * unit_rows, axis=0))


def dot_cols(left, right):
    return lax.dot_general(left, right, CONTRACT_COLS, preferred_element_type=jnp.float32)


def key_blocks(kv_piece, seg_piece, kv_heads, head_size):
    amount = kv_piece.shape[0]
    block_rows = 512
    block_count = amount // block_rows
    key_part = kv_piece[:, : kv_heads * head_size].reshape(
        block_count, block_rows, kv_heads, head_size
    )
    value_part = kv_piece[:, kv_heads * head_size :].reshape(
        block_count, block_rows, kv_heads, head_size
    )
    key_pos = jnp.arange(amount, dtype=jnp.int32).reshape(block_count, block_rows)
    return (key_part, value_part, key_pos, seg_piece.reshape(block_count, block_rows))


def block_scores(queries, key_part, query_pos, query_seg, key_pos, key_seg, scale):
    raw_scores = (
        jnp.einsum("krd,nkd->krn", queries, key_part, preferred_element_type=jnp.float32) * scale
    )
    allowed = (key_pos[None, :] <= query_pos[:, None]) & (key_seg[None, :] == query_seg[:, None])
    return (raw_scores, allowed[None, :, :])


def per_device(
    tokens,
    segment_ids,
    attn_gain,
    w_query,
    b_query,
    w_key,
    b_key,
    w_value,
    b_value,
    w_out,
    ffn_gain,
    w_gate,
    w_up,
    w_down,
    out_grad,
):
    tok_rows, model_width = tokens.shape
    head_size = HD
    kv_heads = w_key.shape[1] // head_size
    query_heads = w_query.shape[1] // head_size
    group_size = query_heads // kv_heads
    group_rows = group_size * tok_rows
    scale = head_size ** (-0.5)
    positions = lax.axis_index("row") * tok_rows + jnp.arange(tok_rows, dtype=jnp.int32)
    cos_table, sin_table = rope_tables(positions.astype(jnp.float32), head_size)
    query_full, key_full, value_full, gate_full, up_full = (
        lax.all_gather(w_query, "row", axis=0, tiled=True),
        lax.all_gather(w_key, "row", axis=0, tiled=True),
        lax.all_gather(w_value, "row", axis=0, tiled=True),
        lax.all_gather(w_gate, "row", axis=0, tiled=True),
        lax.all_gather(w_up, "row", axis=0, tiled=True),
    )
    out_full, down_full = (
        lax.all_gather(w_out, "row", axis=1, tiled=True),
        lax.all_gather(w_down, "row", axis=1, tiled=True),
    )
    inputs = tokens.astype(jnp.float32)
    gain_one = attn_gain.astype(jnp.float32)
    gain_two = ffn_gain.astype(jnp.float32)
    unit_one, inv_one, normed_one = norm_rows(inputs, gain_one)
    normed1 = normed_one.astype(jnp.bfloat16)
    query_lin = (
        jnp.dot(normed1, query_full, preferred_element_type=jnp.float32)
        + b_query.astype(jnp.float32)[None, :]
    )
    key_lin = (
        jnp.dot(normed1, key_full, preferred_element_type=jnp.float32)
        + b_key.astype(jnp.float32)[None, :]
    )
    value_lin = (
        jnp.dot(normed1, value_full, preferred_element_type=jnp.float32)
        + b_value.astype(jnp.float32)[None, :]
    )
    query_rot = rotate(
        query_lin.reshape(tok_rows, query_heads, head_size), cos_table, sin_table
    ).astype(jnp.bfloat16)
    key_rot = rotate(key_lin.reshape(tok_rows, kv_heads, head_size), cos_table, sin_table).astype(
        jnp.bfloat16
    )
    value_rows = value_lin.astype(jnp.bfloat16)
    queries = query_rot.reshape(tok_rows, kv_heads, group_size, head_size).transpose(1, 2, 0, 3)
    queries = queries.reshape(kv_heads, group_rows, head_size)
    query_pos = jnp.tile(positions, group_size)
    query_seg = jnp.tile(segment_ids, group_size)
    kv_send = jnp.concatenate([key_rot.reshape(tok_rows, kv_heads * head_size), value_rows], axis=1)

    def forward_step(state, block_data):
        run_max, run_sum, run_acc = state
        key_part, value_part, key_pos, key_seg = block_data
        raw_scores, allowed = block_scores(
            queries, key_part, query_pos, query_seg, key_pos, key_seg, scale
        )
        masked = jnp.where(allowed, raw_scores, NEG_BIG)
        new_max = jnp.maximum(run_max, jnp.max(masked, axis=2))
        fade = jnp.exp(run_max - new_max)
        weights = jnp.where(allowed, jnp.exp(masked - new_max[:, :, None]), 0.0)
        run_sum = run_sum * fade + jnp.sum(weights, axis=2)
        run_acc = run_acc * fade[:, :, None] + jnp.einsum(
            "krn,nkd->krd",
            weights.astype(jnp.bfloat16),
            value_part,
            preferred_element_type=jnp.float32,
        )
        return ((new_max, run_sum, run_acc), None)

    start_state = (
        jnp.full((kv_heads, group_rows), NEG_BIG, jnp.float32),
        jnp.zeros((kv_heads, group_rows), jnp.float32),
        jnp.zeros((kv_heads, group_rows, head_size), jnp.float32),
    )
    state = start_state
    pieces = (
        lax.all_gather(kv_send, "row", axis=0, tiled=True),
        lax.all_gather(segment_ids, "row", axis=0, tiled=True),
    )
    blocks = key_blocks(pieces[0], pieces[1], kv_heads, head_size)
    state, unused = lax.scan(forward_step, state, blocks)
    run_max, run_sum, run_acc = state
    heads_sum = run_acc / run_sum[:, :, None]
    log_sum = run_max + jnp.log(run_sum)
    attn_heads = heads_sum.reshape(kv_heads, group_size, tok_rows, head_size).transpose(2, 0, 1, 3)
    attn_heads = attn_heads.reshape(tok_rows, query_heads * head_size).astype(jnp.bfloat16)
    attn_branch = lax.psum(
        jnp.dot(attn_heads, out_full, preferred_element_type=jnp.float32).astype(jnp.bfloat16),
        "col",
    ).astype(jnp.float32)
    residual = inputs + attn_branch
    unit_two, inv_two, normed_two = norm_rows(residual, gain_two)
    normed2 = normed_two.astype(jnp.bfloat16)
    gate_lin = jnp.dot(normed2, gate_full, preferred_element_type=jnp.float32)
    up_lin = jnp.dot(normed2, up_full, preferred_element_type=jnp.float32)
    sigmoid_gate = jax.nn.sigmoid(gate_lin)
    silu_gate = gate_lin * sigmoid_gate
    hidden = (silu_gate * up_lin).astype(jnp.bfloat16)
    ffn_branch = lax.psum(
        jnp.dot(hidden, down_full, preferred_element_type=jnp.float32).astype(jnp.bfloat16), "col"
    ).astype(jnp.float32)
    output = (residual + ffn_branch).astype(jnp.bfloat16)
    d_output = out_grad.astype(jnp.float32)
    d_hidden = dot_cols(out_grad, down_full)
    d_gate = (d_hidden * up_lin * sigmoid_gate * (1.0 + gate_lin * (1.0 - sigmoid_gate))).astype(
        jnp.bfloat16
    )
    d_up = (d_hidden * silu_gate).astype(jnp.bfloat16)
    d_normed2 = lax.psum(
        (dot_cols(d_gate, gate_full) + dot_cols(d_up, up_full)).astype(jnp.bfloat16), "col"
    ).astype(jnp.float32)
    d_res_norm, grad_gain_two = norm_back(d_normed2, unit_two, inv_two, gain_two)
    d_residual = d_output + d_res_norm
    d_residual_low = d_residual.astype(jnp.bfloat16)
    d_heads = dot_cols(d_residual_low, out_full).astype(jnp.bfloat16)
    grad_heads = d_heads.reshape(tok_rows, kv_heads, group_size, head_size).transpose(1, 2, 0, 3)
    grad_heads = grad_heads.reshape(kv_heads, group_rows, head_size)
    delta = jnp.sum(grad_heads.astype(jnp.float32) * heads_sum, axis=2)

    def backward_step(dq_acc, block_data):
        key_part, value_part, key_pos, key_seg = block_data
        raw_scores, allowed = block_scores(
            queries, key_part, query_pos, query_seg, key_pos, key_seg, scale
        )
        masked = jnp.where(allowed, raw_scores, NEG_BIG)
        probs = jnp.where(allowed, jnp.exp(masked - log_sum[:, :, None]), 0.0)
        d_probs = jnp.einsum(
            "krd,nkd->krn", grad_heads, value_part, preferred_element_type=jnp.float32
        )
        d_scores = (probs * (d_probs - delta[:, :, None])).astype(jnp.bfloat16)
        dq_acc = (
            dq_acc
            + jnp.einsum("krn,nkd->krd", d_scores, key_part, preferred_element_type=jnp.float32)
            * scale
        )
        d_keys = (
            jnp.einsum("krn,krd->nkd", d_scores, queries, preferred_element_type=jnp.float32)
            * scale
        )
        d_values = jnp.einsum(
            "krn,krd->nkd",
            probs.astype(jnp.bfloat16),
            grad_heads,
            preferred_element_type=jnp.float32,
        )
        amount = key_part.shape[0]
        return (
            dq_acc,
            jnp.concatenate([d_keys.reshape(amount, -1), d_values.reshape(amount, -1)], axis=1),
        )

    pieces = (
        lax.all_gather(kv_send, "row", axis=0, tiled=True),
        lax.all_gather(segment_ids, "row", axis=0, tiled=True),
    )
    dq_acc = jnp.zeros((kv_heads, group_rows, head_size), jnp.float32)
    blocks = key_blocks(pieces[0], pieces[1], kv_heads, head_size)
    dq_acc, dkv_blocks = lax.scan(backward_step, dq_acc, blocks)
    amount = pieces[0].shape[0]
    dkv_piece = dkv_blocks.reshape(amount, -1)
    dkv_all = dkv_piece
    dq_rows, dkv_all = (dq_acc, dkv_all)
    dkv_local = lax.psum_scatter(
        dkv_all.astype(jnp.bfloat16), "row", scatter_dimension=0, tiled=True
    ).astype(jnp.float32)
    dq_rot = dq_rows.reshape(kv_heads, group_size, tok_rows, head_size).transpose(2, 0, 1, 3)
    dq_rot = dq_rot.reshape(tok_rows, query_heads, head_size)
    d_query = rotate(dq_rot, cos_table, -sin_table).reshape(tok_rows, -1).astype(jnp.bfloat16)
    dk_rot = dkv_local[:, : kv_heads * head_size].reshape(tok_rows, kv_heads, head_size)
    d_key = rotate(dk_rot, cos_table, -sin_table).reshape(tok_rows, -1).astype(jnp.bfloat16)
    d_value = dkv_local[:, kv_heads * head_size :].astype(jnp.bfloat16)
    d_normed1 = lax.psum(
        (
            dot_cols(d_query, query_full)
            + dot_cols(d_key, key_full)
            + dot_cols(d_value, value_full)
        ).astype(jnp.bfloat16),
        "col",
    ).astype(jnp.float32)
    d_in_norm, grad_gain_one = norm_back(d_normed1, unit_one, inv_one, gain_one)
    grad_tokens = (d_residual + d_in_norm).astype(jnp.bfloat16)
    qkv_grad = jnp.concatenate([d_query, d_key, d_value], axis=1)
    ffn_grad = jnp.concatenate([d_gate, d_up], axis=1)
    left_cols = (
        lax.all_to_all(normed1, "row", split_axis=1, concat_axis=0, tiled=True),
        lax.all_to_all(normed2, "row", split_axis=1, concat_axis=0, tiled=True),
        lax.all_to_all(d_residual_low, "row", split_axis=1, concat_axis=0, tiled=True),
        lax.all_to_all(out_grad, "row", split_axis=1, concat_axis=0, tiled=True),
    )
    pieces = (
        lax.all_gather(qkv_grad, "row", axis=0, tiled=True),
        lax.all_gather(ffn_grad, "row", axis=0, tiled=True),
        lax.all_gather(attn_heads, "row", axis=0, tiled=True),
        lax.all_gather(hidden, "row", axis=0, tiled=True),
    )
    partial_grads = tuple(
        (
            lax.dot_general(left, piece, CONTRACT_ROWS, preferred_element_type=jnp.float32)
            for left, piece in zip(left_cols, pieces)
        )
    )
    qkv_sum, ffn_sum, heads_grad, hidden_grad = jax.tree.map(
        lambda part: part.astype(jnp.float32), lax.psum(shortened(partial_grads), "dp")
    )
    grad_b_query, grad_b_key, grad_b_value, grad_attn_gain, grad_ffn_gain = lax.psum(
        (
            jnp.sum(d_query, axis=0, dtype=jnp.float32),
            jnp.sum(d_key, axis=0, dtype=jnp.float32),
            jnp.sum(d_value, axis=0, dtype=jnp.float32),
            grad_gain_one,
            grad_gain_two,
        ),
        ("dp", "row"),
    )
    query_width = query_heads * head_size
    kv_width = kv_heads * head_size
    ffn_width = gate_full.shape[1]
    grad_w_query = qkv_sum[:, :query_width]
    grad_w_key = qkv_sum[:, query_width : query_width + kv_width]
    grad_w_value = qkv_sum[:, query_width + kv_width :]
    grad_w_gate = ffn_sum[:, :ffn_width]
    grad_w_up = ffn_sum[:, ffn_width:]
    grad_w_out = heads_grad.T
    grad_w_down = hidden_grad.T
    return (
        output,
        grad_tokens,
        grad_attn_gain,
        grad_w_query,
        grad_b_query,
        grad_w_key,
        grad_b_key,
        grad_w_value,
        grad_b_value,
        grad_w_out,
        grad_ffn_gain,
        grad_w_gate,
        grad_w_up,
        grad_w_down,
    )


def solution(mesh):
    return jax.shard_map(
        per_device,
        mesh=mesh,
        in_specs=(
            P(("dp", "row"), None),
            P(("dp", "row")),
            P(),
            P("row", "col"),
            P("col"),
            P("row", "col"),
            P("col"),
            P("row", "col"),
            P("col"),
            P("col", "row"),
            P(),
            P("row", "col"),
            P("row", "col"),
            P("col", "row"),
            P(("dp", "row"), None),
        ),
        out_specs=(
            P(("dp", "row"), None),
            P(("dp", "row"), None),
            P(),
            P("row", "col"),
            P("col"),
            P("row", "col"),
            P("col"),
            P("row", "col"),
            P("col"),
            P("col", "row"),
            P(),
            P("row", "col"),
            P("row", "col"),
            P("col", "row"),
        ),
        check_vma=False,
    )
```

profile of v0, /device:TPU:0, one launch (start us, length us, event | category | flops | bytes accessed | tf_op | source)
XLA Modules:
  0.0 935.9 jit_solution(17343965434470648157)
XLA Ops:
  9.3 12.8 %all-gather = s32[4,1,256]{2,1,0:T(1,128)S(1)} all-gather(s32[1,1,256]{2,1,0:T(1,128)} %bitcast), channel_id=1, replica_groups=mesh['dp'=4,'row'=4,'col'=2] {'row'}, dimensions={0}, use_global_device_ids=true | all-gather | bytes 5120 | tf_op jit(solution)/shard_map/all_gather | solution.py:174
  23.5 1.2 fusion.73
  24.7 13.6 %all-gather.2 = bf16[4,224,64]{1,2,0:T(8,128)(2,1)S(1)} all-gather(bf16[1,224,64]{1,2,0:T(8,128)(2,1)} %bitcast.241), channel_id=1, replica_groups=mesh['dp'=4,'row'=4,'col'=2] {'row'}, dimensions={0}, use_global_device_ids=true | all-gather | bytes 143360 | tf_op jit(solution)/shard_map/all_gather | solution.py:109
  39.2 13.6 %all-gather.1 = bf16[4,224,64]{1,2,0:T(8,128)(2,1)S(1)} all-gather(bf16[1,224,64]{1,2,0:T(8,128)(2,1)} %bitcast.242), channel_id=1, replica_groups=mesh['dp'=4,'row'=4,'col'=2] {'row'}, dimensions={0}, use_global_device_ids=true | all-gather | bytes 143360 | tf_op jit(solution)/shard_map/all_gather | solution.py:108
  53.7 1.2 fusion.70
  56.5 14.7 %all_gather.44 = bf16[1024,128]{0,1:T(8,128)(2,1)S(1)} all-gather(bf16[256,128]{0,1:T(8,128)(2,1)S(1)} %pad_maximum_fusion.2), channel_id=1, replica_groups=mesh['dp'=4,'row'=4,'col'=2] {'row'}, dimensions={0}, use_global_device_ids=true | all-gather | bytes 327680 | tf_op jit(solution)/shard_map/all_gather | solution.py:173
  72.0 16.1 %all_gather.45 = bf16[896,448]{1,0:T(8,128)(2,1)S(1)} all-gather(bf16[224,448]{1,0:T(8,128)(2,1)S(1)} %copy-done.35), channel_id=1, replica_groups=mesh['dp'=4,'row'=4,'col'=2] {'row'}, dimensions={0}, use_global_device_ids=true | all-gather | bytes 1003520 | tf_op jit(solution)/shard_map/all_gather | solution.py:107
  89.5 12.8 %while.28 = (s32[]{:T(128)}, f32[1,1792]{1,0:T(1,128)S(1)}, f32[1,1792]{1,0:T(1,128)S(1)}, f32[1,1792,64]{1,2,0:T(8,128)S(1)}, s32[2,512]{1,0:T(2,128)}, /*index...) while((s32[]{:T(128)}, f32[1,1792]{1,0:T(1,128)S(1)}, ...), condition=%wide.region_4.5_spmd.clone, body=%wide.region_1.4_spmd.clone.sunk | while | flops 251750912 | bytes 12522653 | solution.py:177
  91.6 2.0 fusion.176
  98.0 2.0 fusion.176
  104.1 16.0 %all_gather.46 = bf16[448,896]{0,1:T(8,128)(2,1)S(1)} all-gather(bf16[448,224]{0,1:T(8,128)(2,1)S(1)} %copy.187), channel_id=1, replica_groups=mesh['dp'=4,'row'=4,'col'=2] {'row'}, dimensions={1}, use_global_device_ids=true | all-gather | bytes 1003520 | tf_op jit(solution)/shard_map/all_gather | solution.py:114
  120.1 1.2 convolution_convert_fusion.3
  123.4 15.7 %all-reduce.8.cloned.1.call-done = bf16[256,896]{1,0:T(8,128)(2,1)} async-done(((bf16[256,896]{1,0:T(8,128)(2,1)}), bf16[256,896]{1,0:T(8,128)(2,1)}) %all-reduce.8.cloned.1.call-update) | async-done | bytes 458768 | tf_op jit(solution)/shard_map/psum | solution.py:183
  139.1 1.2 multiply_reduce_fusion
  140.4 1.2 multiply_convert_fusion.3
  141.6 64.2 %all-gather.10.cloned.1.call-done = bf16[896,2432]{1,0:T(8,128)(2,1)} async-done(((bf16[224,2432]{1,0:T(8,128)(2,1)}), bf16[896,2432]{1,0:T(8,128)(2,1)}) %all-gather.10.cloned.1.call-update) | async-done | bytes 4358160 | tf_op jit(solution)/shard_map/all_gather | solution.py:110
  205.8 5.2 fusion.112
  211.0 78.2 %all-gather.12.cloned.1.call-done = bf16[896,2432]{1,0:T(8,128)(2,1)} async-done(((bf16[224,2432]{1,0:T(8,128)(2,1)}), bf16[896,2432]{1,0:T(8,128)(2,1)}) %all-gather.12.cloned.1.call-update) | async-done | bytes 4358160 | tf_op jit(solution)/shard_map/all_gather | solution.py:111
  289.2 5.2 fusion.113
  294.4 78.1 %all-gather.14.cloned.1.call-done = bf16[2432,896]{0,1:T(8,128)(2,1)} async-done(((bf16[2432,224]{0,1:T(8,128)(2,1)}), bf16[2432,896]{0,1:T(8,128)(2,1)}) %all-gather.14.cloned.1.call-update) | async-done | bytes 4358160 | tf_op jit(solution)/shard_map/all_gather | solution.py:115
  372.5 6.5 multiply_convert_fusion
  379.0 4.7 fusion.114
  383.8 2.3 fusion.56
  386.4 17.0 %all-reduce.10.cloned.1.call-done = bf16[256,896]{1,0:T(8,128)(2,1)} async-done(((bf16[256,896]{1,0:T(8,128)(2,1)}), bf16[256,896]{1,0:T(8,128)(2,1)}) %all-reduce.10.cloned.1.call-update) | async-done | bytes 458768 | tf_op jit(solution)/shard_map/psum | solution.py:205
  403.4 2.1 fusion.69
  405.5 1.4 fusion.105
  409.7 34.4 %while.29 = (s32[]{:T(128)}, f32[1,1792,64]{1,2,0:T(8,128)}, bf16[2,512,128]{1,2,0:T(8,128)(2,1)}, s32[2,512]{1,0:T(2,128)}, s32[2,512]{1,0:T(2,128)}, /*index=5...) while((s32[]{:T(128)}, f32[1,1792,64]{1,2,0:T(8,128)}, ...), condition=%wide.region_12.13_spmd.clone, body=%wide.region_11.12_spmd.clone.sunk | while | flops 597966848 | bytes 21153020 | solution.py:254
  412.5 4.0 fusion.191
  416.5 1.3 reduce.22
  417.8 2.7 fusion.192
  420.6 2.1 fusion.193
  422.6 2.8 fusion.194
  429.6 4.0 fusion.191
  433.6 1.3 reduce.22
  434.9 2.7 fusion.192
  437.7 2.3 fusion.193
  440.0 2.8 fusion.194
  444.1 1.8 copy.210
  446.0 1.2 reshape.441
  448.8 18.1 %reduce-scatter.2.cloned.1.call-done = bf16[256,128]{0,1:T(8,128)(2,1)} async-done(((bf16[1024,128]{0,1:T(8,128)(2,1)}), bf16[256,128]{0,1:T(8,128)(2,1)}) %reduce-scatter.2.cloned.1.call-update) | async-done | bytes 65552 | tf_op jit(solution)/shard_map/reduce_scatter | solution.py:259
  469.6 3.0 pad_maximum_fusion
  473.6 3.5 all-to-all-start
  478.1 21.4 %all-to-all-done = bf16[256,4,224]{0,2,1:T(8,128)(2,1)S(1)} async-done(((bf16[256,4,224]{0,2,1:T(8,128)(2,1)}), bf16[256,4,224]{0,2,1:T(8,128)(2,1)S(1)}, u32[]{:S(2)}, u32[]{:S(2)}) %all-to-all-start) | async-done | bytes 458784 | tf_op jit(solution)/shard_map/all_to_all | solution.py:281
  499.5 6.2 all-to-all-start.3
  506.7 11.3 %all-to-all-done.3 = bf16[256,4,224]{0,2,1:T(8,128)(2,1)S(1)} async-done(((bf16[256,4,224]{0,2,1:T(8,128)(2,1)}), bf16[256,4,224]{0,2,1:T(8,128)(2,1)S(1)}, u32[]{:S(2)}, u32[]{:S(2)}) %all-to-all-start.3) | async-done | bytes 458784 | tf_op jit(solution)/shard_map/all_to_all | solution.py:284
  517.9 3.5 all-to-all-start.2
  521.4 50.8 %all_gather.51 = bf16[1024,448]{0,1:T(8,128)(2,1)S(1)} all-gather(bf16[256,448]{0,1:T(8,128)(2,1)S(1)} %bitcast.215), channel_id=1, replica_groups=mesh['dp'=4,'row'=4,'col'=2] {'row'}, dimensions={0}, use_global_device_ids=true | all-gather | bytes 1146880 | tf_op jit(solution)/shard_map/all_gather | solution.py:289
  574.7 5.0 convolution_convert_fusion.2
  580.7 6.4 all-to-all-start.1
  587.6 1.2 convolution_add_fusion.1
  590.3 21.7 %all-to-all-done.1 = bf16[256,4,224]{0,2,1:T(8,128)(2,1)S(1)} async-done(((bf16[256,4,224]{0,2,1:T(8,128)(2,1)}), bf16[256,4,224]{0,2,1:T(8,128)(2,1)S(1)}, u32[]{:S(2)}, u32[]{:S(2)}) %all-to-all-start.1) | async-done | bytes 458784 | tf_op jit(solution)/shard_map/all_to_all | solution.py:283
  613.2 2.8 convolution_convert_fusion.4
  615.9 21.6 %all-gather.20.cloned.1.call-done = bf16[1024,2432]{1,0:T(8,128)(2,1)} async-done(((bf16[256,2432]{1,0:T(8,128)(2,1)}), bf16[1024,2432]{1,0:T(8,128)(2,1)}) %all-gather.20.cloned.1.call-update) | async-done | bytes 4980752 | tf_op jit(solution)/shard_map/all_gather | solution.py:290
  637.5 4.8 convolution_convert_fusion.1
  642.3 171.1 %all-gather.18.cloned.1.call-done = bf16[1024,4864]{1,0:T(8,128)(2,1)} async-done(((bf16[256,4864]{1,0:T(8,128)(2,1)}), bf16[1024,4864]{1,0:T(8,128)(2,1)}) %all-gather.18.cloned.1.call-update) | async-done | bytes 9961488 | tf_op jit(solution)/shard_map/all_gather | solution.py:288
  813.4 7.6 convolution_convert_fusion
  822.2 1.5 fusion.72
  823.7 75.2 %all-reduce = (f32[896]{0:T(1024)}, f32[448]{0:T(512)}, f32[64]{0:T(128)}, f32[64]{0:T(128)}, f32[896]{0:T(1024)}) all-reduce(f32[896]{0:T(1024)S(1)} %get-tuple-element.506, f32[448]{0:T(512)S(1)} %reduce_sum.113, f32[64]{0:T(128)S(1)} %convert_reduce_fusion.2, ...), channel_id=1, replica_groups=mesh['dp'=4,'row'=4,'col'=2] {'dp','row'}, use_global_device_ids=true, to_apply=%region_17.18 | all-reduce | flops 2368 | bytes 18944 | tf_op jit(solution)/shard_map/psum | solution.py:301
  898.9 2.8 fusion.65
  901.8 17.1 %all-reduce.12.cloned.1.call-done = (bf16[224,576]{1,0:T(8,128)(2,1)}, bf16[448,224]{0,1:T(8,128)(2,1)}, bf16[224,4864]{1,0:T(8,128)(2,1)}, bf16[2432,224]{0,1:T(8,128)(2,1)}) async-done(((bf16[224,576]{1,0:T(8,128)(2,1)}, bf16[448,224]{0,1:T(8,128)(2,1)}, bf16[224,4864]{1,0:T(8,128)(2,1)}, bf16[2432,224]{0,1:T(8,128)(2,1)}), (bf16[224,576]{1,0:T(8,128)(2,1)}, bf16[448,224]{0,1:T(8,128)(2,1)}, ...) | async-done | bytes 3727376 | tf_op jit(solution)/shard_map/psum | solution.py:299
  918.8 1.9 slice.84
  923.1 1.8 copy.206
  924.9 2.3 fusion.107
  927.3 1.5 transpose.91
  (252 shorter events, 49.3 us)
Async XLA Ops:
  8.0 64.0 %copy-start.35 = (bf16[224,448]{1,0:T(8,128)(2,1)S(1)}, bf16[224,448]{1,0:T(8,128)(2,1)}, u32[]{:S(2)}) copy-start(bf16[224,448]{1,0:T(8,128)(2,1)} %param.22) | copy-start | bytes 602116
  8.0 80.1 %copy-start.54 = (bf16[448]{0:T(512)(128)(2,1)S(1)}, bf16[448]{0:T(512)(128)(2,1)}, u32[]{:S(2)}) copy-start(bf16[448]{0:T(512)(128)(2,1)} %param.23) | copy-start | bytes 2692
  8.0 131.1 %all-reduce.8.cloned.1.call-start = ((), (), s32[]{:S(2)}) async-start(), calls=%async_computation.5 | async-start | bytes 917504 | tf_op jit(solution)/shard_map/psum | solution.py:183
  8.7 47.3 %copy-start.51 = (f32[32]{0:T(128)}, f32[32]{0:T(128)S(1)}, u32[]{:S(2)}) copy-start(f32[32]{0:T(128)S(1)} %multiply_exponential_fusion) | copy-start | bytes 388
  8.7 47.3 %copy-start.47 = (f32[256]{0:T(256)}, f32[256]{0:T(256)S(1)}, u32[]{:S(2)}) copy-start(f32[256]{0:T(256)S(1)} %fusion.103) | copy-start | bytes 3076
  23.5 30.2 %copy-start.40 = (f32[896]{0:T(1024)}, f32[896]{0:T(1024)S(1)}, u32[]{:S(2)}) copy-start(f32[896]{0:T(1024)S(1)} %convert_element_type.182) | copy-start | bytes 10756
  24.7 29.0 %copy-start.45 = (f32[256]{0:T(256)}, f32[256]{0:T(256)S(1)}, u32[]{:S(2)}) copy-start(f32[256]{0:T(256)S(1)} %add_rsqrt_fusion.1) | copy-start | bytes 3076
  53.0 35.7 %copy-start.22 = (bf16[896,64]{0,1:T(8,128)(2,1)}, bf16[896,64]{0,1:T(8,128)(2,1)S(1)}, u32[]{:S(2)}) copy-start(bf16[896,64]{0,1:T(8,128)(2,1)S(1)} %reshape.450) | copy-start | bytes 344068
  54.9 34.1 %copy-start.1 = (bf16[256,896]{1,0:T(8,128)(2,1)}, bf16[256,896]{1,0:T(8,128)(2,1)S(1)}, u32[]{:S(2)}) copy-start(bf16[256,896]{1,0:T(8,128)(2,1)S(1)} %fusion.70) | copy-start | bytes 1376260
  55.7 33.3 %copy-start.25 = (f32[256,32]{0,1:T(8,128)}, f32[256,32]{0,1:T(8,128)S(1)}, u32[]{:S(2)}) copy-start(f32[256,32]{0,1:T(8,128)S(1)} %get-tuple-element.603) | copy-start | bytes 98308
  89.5 14.5 %copy-start.34 = (bf16[448,224]{1,0:T(8,128)(2,1)S(1)}, bf16[448,224]{1,0:T(8,128)(2,1)}, u32[]{:S(2)}) copy-start(bf16[448,224]{1,0:T(8,128)(2,1)} %param.28) | copy-start | bytes 602116
  102.3 1.6 copy-start.17
  103.9 19.5 %copy-start.53 = (bf16[896]{0:T(1024)(128)(2,1)S(1)}, bf16[896]{0:T(1024)(128)(2,1)}, u32[]{:S(2)}) copy-start(bf16[896]{0:T(1024)(128)(2,1)} %param.29) | copy-start | bytes 5380
  103.9 35.2 %copy-start = (bf16[256,896]{1,0:T(8,128)(2,1)S(1)}, bf16[256,896]{1,0:T(8,128)(2,1)}, u32[]{:S(2)}) copy-start(bf16[256,896]{1,0:T(8,128)(2,1)} %param.19) | copy-start | bytes 1376260
  121.4 84.4 %all-gather.10.cloned.1.call-start = ((), (), s32[]{:S(2)}) async-start(), calls=%async_computation.6 | async-start | bytes 5447680 | tf_op jit(solution)/shard_map/all_gather | solution.py:110
  122.0 167.2 %all-gather.12.cloned.1.call-start = ((), (), s32[]{:S(2)}) async-start(), calls=%async_computation.7 | async-start | bytes 5447680 | tf_op jit(solution)/shard_map/all_gather | solution.py:111
  122.6 249.9 %all-gather.14.cloned.1.call-start = ((), (), s32[]{:S(2)}) async-start(), calls=%async_computation.8 | async-start | bytes 5447680 | tf_op jit(solution)/shard_map/all_gather | solution.py:115
  123.2 280.2 %all-reduce.10.cloned.1.call-start = ((), (), s32[]{:S(2)}) async-start(), calls=%async_computation.9 | async-start | bytes 917504 | tf_op jit(solution)/shard_map/psum | solution.py:205
  123.4 82.4 %copy-start.37 = (f32[896]{0:T(1024)}, f32[896]{0:T(1024)S(1)}, u32[]{:S(2)}) copy-start(f32[896]{0:T(1024)S(1)} %convert_element_type.195) | copy-start | bytes 10756
  140.4 65.4 %copy-start.42 = (f32[256]{0:T(256)}, f32[256]{0:T(256)S(1)}, u32[]{:S(2)}) copy-start(f32[256]{0:T(256)S(1)} %add_rsqrt_fusion) | copy-start | bytes 3076
  141.6 147.6 %copy-start.15 = (bf16[256,896]{1,0:T(8,128)(2,1)}, bf16[256,896]{1,0:T(8,128)(2,1)S(1)}, u32[]{:S(2)}) copy-start(bf16[256,896]{1,0:T(8,128)(2,1)S(1)} %multiply_convert_fusion.3) | copy-start | bytes 1376260
  211.0 161.5 %copy-start.8 = (bf16[256,896]{1,0:T(8,128)(2,1)S(1)}, bf16[256,896]{1,0:T(8,128)(2,1)}, u32[]{:S(2)}) copy-start(bf16[256,896]{1,0:T(8,128)(2,1)} %param.33) | copy-start | bytes 1376260
  379.0 4.7 copy-start.20
  379.0 4.8 copy-start.18
  379.0 4.8 copy-start.55
  383.8 19.6 %copy-start.3 = (bf16[256,896]{1,0:T(8,128)(2,1)S(1)}, bf16[256,896]{1,0:T(8,128)(2,1)}, u32[]{:S(2)}) copy-start(bf16[256,896]{1,0:T(8,128)(2,1)} %all-reduce.8.cloned.1.call-done) | copy-start | bytes 1376260
  386.1 80.8 %reduce-scatter.2.cloned.1.call-start = ((), (), s32[]{:S(2)}) async-start(), calls=%async_computation.10 | async-start | bytes 327680 | tf_op jit(solution)/shard_map/reduce_scatter | solution.py:259
  405.5 2.3 copy-start.49
  422.6 3.4 copy-start.32
  439.9 3.4 copy-start.32
  444.1 23.6 %copy-start.48 = (f32[256]{0:T(256)S(1)}, f32[256]{0:T(256)}, u32[]{:S(2)}) copy-start(f32[256]{0:T(256)} %copy-done.47) | copy-start | bytes 3076
  444.1 23.6 %copy-start.52 = (f32[32]{0:T(128)S(1)}, f32[32]{0:T(128)}, u32[]{:S(2)}) copy-start(f32[32]{0:T(128)} %copy-done.51) | copy-start | bytes 388
  444.1 25.4 %copy-start.19 = (bf16[256,2432]{1,0:T(8,128)(2,1)S(1)}, bf16[256,2432]{1,0:T(8,128)(2,1)}, u32[]{:S(2)}) copy-start(bf16[256,2432]{1,0:T(8,128)(2,1)} %copy-done.18) | copy-start | bytes 3735556
  445.9 167.2 %all-gather.16.cloned.1.call-start = ((), (), s32[]{:S(2)}) async-start(), calls=%async_computation.11 | async-start | bytes 1474560 | tf_op jit(solution)/shard_map/all_gather | solution.py:287
  448.8 20.0 %copy-start.13 = (bf16[256,7,64]{0,2,1:T(8,128)(2,1)}, bf16[256,7,64]{0,2,1:T(8,128)(2,1)S(1)}, u32[]{:S(2)}) copy-start(bf16[256,7,64]{0,2,1:T(8,128)(2,1)S(1)} %copy.193) | copy-start | bytes 688132
  467.9 4.7 copy-start.26
  467.9 4.7 copy-start.28
  468.8 168.8 %all-gather.20.cloned.1.call-start = ((), (), s32[]{:S(2)}) async-start(), calls=%async_computation.13 | async-start | bytes 6225920 | tf_op jit(solution)/shard_map/all_gather | solution.py:290
  469.5 3.2 copy-start.2
  469.5 7.6 copy-start.9
  469.5 343.9 %all-gather.18.cloned.1.call-start = ((), (), s32[]{:S(2)}) async-start(), calls=%async_computation.12 | async-start | bytes 12451840 | tf_op jit(solution)/shard_map/all_gather | solution.py:288
  472.6 33.1 %copy-start.16 = (bf16[256,896]{1,0:T(8,128)(2,1)S(1)}, bf16[256,896]{1,0:T(8,128)(2,1)}, u32[]{:S(2)}) copy-start(bf16[256,896]{1,0:T(8,128)(2,1)} %copy-done.15) | copy-start | bytes 1376260
  473.6 25.9 %all-to-all-start = ((bf16[256,4,224]{0,2,1:T(8,128)(2,1)}), bf16[256,4,224]{0,2,1:T(8,128)(2,1)S(1)}, u32[]{:S(2)}, u32[]{:S(2)}) async-start(bf16[256,4,224]{0,2,1:T(8,128)(2,1)} %bitcast.21), calls=%async_computation.1 | async-start | bytes 917504 | tf_op jit(solution)/shard_map/all_to_all | solution.py:281
  499.5 18.4 %all-to-all-start.3 = ((bf16[256,4,224]{0,2,1:T(8,128)(2,1)}), bf16[256,4,224]{0,2,1:T(8,128)(2,1)S(1)}, u32[]{:S(2)}, u32[]{:S(2)}) async-start(bf16[256,4,224]{0,2,1:T(8,128)(2,1)} %bitcast.28), calls=%async_computation.4 | async-start | bytes 917504 | tf_op jit(solution)/shard_map/all_to_all | solution.py:284
  517.9 55.9 %all-to-all-start.2 = ((bf16[256,4,224]{0,2,1:T(8,128)(2,1)}), bf16[256,4,224]{0,2,1:T(8,128)(2,1)S(1)}, u32[]{:S(2)}, u32[]{:S(2)}) async-start(bf16[256,4,224]{0,2,1:T(8,128)(2,1)} %bitcast.26), calls=%async_computation.3 | async-start | bytes 917504 | tf_op jit(solution)/shard_map/all_to_all | solution.py:282
  574.7 5.1 copy-start.11
  574.7 12.4 %copy-start.7 = (bf16[896,448]{1,0:T(8,128)(2,1)S(1)}, bf16[896,448]{1,0:T(8,128)(2,1)}, u32[]{:S(2)}) copy-start(bf16[896,448]{1,0:T(8,128)(2,1)} %copy-done.6) | copy-start | bytes 2408452
  574.7 12.4 %copy-start.14 = (bf16[256,7,64]{0,2,1:T(8,128)(2,1)S(1)}, bf16[256,7,64]{0,2,1:T(8,128)(2,1)}, u32[]{:S(2)}) copy-start(bf16[256,7,64]{0,2,1:T(8,128)(2,1)} %copy-done.13) | copy-start | bytes 688132
  580.7 31.3 %all-to-all-start.1 = ((bf16[256,4,224]{0,2,1:T(8,128)(2,1)}), bf16[256,4,224]{0,2,1:T(8,128)(2,1)S(1)}, u32[]{:S(2)}, u32[]{:S(2)}) async-start(bf16[256,4,224]{0,2,1:T(8,128)(2,1)} %bitcast.220), calls=%async_computation.2 | async-start | bytes 917504 | tf_op jit(solution)/shard_map/all_to_all | solution.py:283
  587.1 235.0 %all-reduce.14.cloned.1.call-start = ((), (), s32[]{:S(2)}) async-start(), calls=%async_computation.15 | async-start | bytes 1835008 | tf_op jit(solution)/shard_map/psum | solution.py:195
  587.1 1.7 copy-start.30
  589.9 47.6 %copy-start.23 = (bf16[4,28,8,256]{3,2,0,1:T(8,128)(2,1)S(1)}, bf16[4,28,8,256]{3,2,0,1:T(8,128)(2,1)}, u32[]{:S(2)}) copy-start(bf16[4,28,8,256]{3,2,0,1:T(8,128)(2,1)} %copy.214) | copy-start | bytes 1376260
  590.0 328.9 %all-reduce.12.cloned.1.call-start = ((), (), s32[]{:S(2)}) async-start(), calls=%async_computation.14 | async-start | bytes 7569408 | tf_op jit(solution)/shard_map/psum | solution.py:299
  615.9 197.5 %copy-start.24 = (bf16[4,28,8,256]{3,2,0,1:T(8,128)(2,1)S(1)}, bf16[4,28,8,256]{3,2,0,1:T(8,128)(2,1)}, u32[]{:S(2)}) copy-start(bf16[4,28,8,256]{3,2,0,1:T(8,128)(2,1)} %copy.213) | copy-start | bytes 1376260
  821.0 1.2 copy-start.41
  821.0 1.2 copy-start.46
  821.0 2.7 copy-start.44
  821.0 77.9 %copy-start.4 = (bf16[256,896]{1,0:T(8,128)(2,1)S(1)}, bf16[256,896]{1,0:T(8,128)(2,1)}, u32[]{:S(2)}) copy-start(bf16[256,896]{1,0:T(8,128)(2,1)} %all-reduce.8.cloned.1.call-done) | copy-start | bytes 1376260
  821.0 77.9 %copy-start.12 = (bf16[256,896]{1,0:T(8,128)(2,1)S(1)}, bf16[256,896]{1,0:T(8,128)(2,1)}, u32[]{:S(2)}) copy-start(bf16[256,896]{1,0:T(8,128)(2,1)} %all-reduce.10.cloned.1.call-done) | copy-start | bytes 1376260
  821.0 77.9 %copy-start.38 = (f32[896]{0:T(1024)S(1)}, f32[896]{0:T(1024)}, u32[]{:S(2)}) copy-start(f32[896]{0:T(1024)} %copy-done.37) | copy-start | bytes 10756
  821.0 77.9 %copy-start.43 = (f32[256]{0:T(256)S(1)}, f32[256]{0:T(256)}, u32[]{:S(2)}) copy-start(f32[256]{0:T(256)} %copy-done.42) | copy-start | bytes 3076
  821.1 77.9 %copy-start.50 = (f32[256]{0:T(256)S(1)}, f32[256]{0:T(256)}, u32[]{:S(2)}) copy-start(f32[256]{0:T(256)} %copy-done.49) | copy-start | bytes 3076
  918.8 6.1 copy-start.5
  924.9 2.3 copy-start.21
  (9 other events, 7.3 us)
Sparse Core Ops, SparseCore 0:
  121.5 17.5 all-reduce.7
  386.2 17.0 all-reduce.9
  591.6 21.0 all-reduce.13
  821.2 97.5 all-reduce.11
Sparse Core Ops, SparseCore 1:
  123.5 82.2 all-gather.9
  207.3 81.8 all-gather.11
  290.7 81.8 all-gather.13
  446.0 20.9 reduce-scatter.1
  468.8 38.6 all-gather.15
  509.6 127.8 all-gather.19
  638.9 174.4 all-gather.17
where the time goes:
time: 938 us; the launch traced here: 936 us
  waiting for transfers between devices  538 us (57%)
  blocking collectives  213 us (23%)
  matrix products  81.8 us (9%)
  local copies, waits for them, and re-layouts  33.5 us (4%)
  other arithmetic  33.1 us (4%)
  starting transfers between devices  20.6 us (2%)
  between operations  16.1 us (2%)
    all_gather x1, waiting for transfers between devices, per_device(): lax.all_gather(ffn_grad, 'row', axis=0, tiled=True)  171 us
    all_gather x1, waiting for transfers between devices, per_device(): lax.all_gather(w_up, 'row', axis=0, tiled=True)  78.2 us
    all_gather x1, waiting for transfers between devices, per_device(): lax.all_gather(w_down, 'row', axis=1, tiled=True)  78.1 us
    psum x1, blocking collectives, per_device(): lax.psum((jnp.sum(d_query, axis=0, dtype=jnp.float32), jnp.sum(d_key, axi...  75.2 us
    all_gather x1, waiting for transfers between devices, per_device(): lax.all_gather(w_gate, 'row', axis=0, tiled=True)  64.2 us
    all_gather x1, blocking collectives, per_device(): lax.all_gather(attn_heads, 'row', axis=0, tiled=True)  50.8 us
    all_to_all x1, waiting for transfers between devices, per_device(): lax.all_to_all(d_residual_low, 'row', split_axis=1, concat_axis=0, tiled=...  21.7 us
    all_gather x1, waiting for transfers between devices, per_device(): lax.all_gather(hidden, 'row', axis=0, tiled=True)  21.6 us
  transfers between devices with their start and end apart: 15, of which 12 were waited for; matrix products, arithmetic and copies ran while one was open for 6% of the time, Pallas kernels for 0%

commit v1 on v0

v1 whole, which is shorter than its diff:
```python
import functools

import jax
import jax.numpy as jnp
from jax import lax
from jax.experimental import pallas as pl
from jax.experimental.pallas import tpu as pltpu
from jax.sharding import PartitionSpec as P

HD = 64
HALF = HD // 2
NORM_EPS = 1e-06
ROPE_BASE = 1000000.0
NEG_BIG = -1e30
LANES = 128
EXTRA_ROWS = 16
BF16 = jnp.bfloat16
F32 = jnp.float32


def dot_rows(left, right):
    return lax.dot_general(left, right, (((0,), (0,)), ((), ())), preferred_element_type=F32)


def dot_cols(left, right):
    return lax.dot_general(left, right, (((1,), (1,)), ((), ())), preferred_element_type=F32)


def dot(left, right):
    return jnp.dot(left, right, preferred_element_type=F32)


def inverse_rms(values):
    return lax.rsqrt(jnp.mean(values * values, axis=1, keepdims=True) + NORM_EPS)


def norm_back(gradient, unit_rows, inv_rms, gain):
    scaled = gradient * gain
    inner = jnp.mean(scaled * unit_rows, axis=1, keepdims=True)
    return (inv_rms * (scaled - unit_rows * inner), jnp.sum(gradient * unit_rows, axis=0))


def swap_core(value):
    return lax.ppermute(value, "col", [(0, 1), (1, 0)])


def dp_step(value, step):
    pairs = []
    for group in range(4):
        for core in range(2):
            bit = 1 << ((step + core) % 2)
            pairs.append((group * 2 + core, (group ^ bit) * 2 + core))
    return lax.ppermute(value, ("dp", "col"), pairs)


def dp_gather(value):
    first = dp_step(value, 0)
    pair = jnp.stack([value, first])
    second = dp_step(pair, 1)
    return jnp.concatenate([pair, second], axis=0)


def dp_scatter_sum(parts):
    first = dp_step(parts[2:].astype(BF16), 1)
    pair = parts[:2] + first.astype(F32)
    second = dp_step(pair[1].astype(BF16), 0)
    return pair[0] + second.astype(F32)


def dp_scatter_sum_cols(parts):
    kept = parts[0::2].astype(F32)
    pair = kept + dp_step(parts[1::2], 0).astype(F32)
    return pair[0] + dp_step(pair[1].astype(BF16), 1).astype(F32)


def dp_exchange(parts):
    first = dp_step(parts[1::2], 0)
    kept = jnp.stack([parts[0], first[0]])
    onward = jnp.stack([parts[2], first[1]])
    return jnp.concatenate([kept, dp_step(onward, 1)], axis=0)


def dp_slots(group, core):
    slots = []
    for j in range(4):
        relative = group ^ j
        flipped = (relative & 1) * 2 + (relative >> 1)
        slots.append(jnp.where(core == 0, relative, flipped))
    return slots


def pick(stacked, place, axis=0):
    return lax.dynamic_index_in_dim(stacked, place, axis=axis, keepdims=False)


def half_turn(values):
    lane = lax.broadcasted_iota(jnp.int32, values.shape, 1) % HD
    return jnp.where(lane < HALF, -jnp.roll(values, -HALF, axis=1), jnp.roll(values, HALF, axis=1))


def mask_bias(q_meta, k_meta):
    allowed = (k_meta[0:1, :] <= q_meta[:, 0:1]) & (k_meta[1:2, :] == q_meta[:, 1:2])
    return jnp.where(allowed, 0.0, NEG_BIG)


def attend_kernel(heads, q_ref, kv_ref, qm_ref, km_ref, out_ref, lse_ref, bias_ref):
    bias_ref[...] = mask_bias(qm_ref[...], km_ref[...])
    keys = kv_ref[:, :HD]
    values = kv_ref[:, HD:]
    lane = lax.broadcasted_iota(jnp.int32, lse_ref.shape, 1)
    lse_all = jnp.zeros(lse_ref.shape, F32)
    outs = []
    for head in range(heads):
        cols = slice(head * HD, (head + 1) * HD)
        scores = dot_cols(q_ref[:, cols], keys) + bias_ref[...]
        top = jnp.max(scores, axis=1, keepdims=True)
        weights = jnp.exp(scores - top)
        total = jnp.sum(weights, axis=1, keepdims=True)
        outs.append(dot(weights.astype(BF16), values) / total)
        lse_all = jnp.where(lane == head, top + jnp.log(total), lse_all)
    out_ref[...] = jnp.concatenate(outs, axis=1)
    lse_ref[...] = lse_all


def attend_back_kernel(
    heads, q_ref, kv_ref, qm_ref, km_ref, out_ref, lse_ref, do_ref, dq_ref, dkv_ref, bias_ref
):
    bias_ref[...] = mask_bias(qm_ref[...], km_ref[...])
    keys = kv_ref[:, :HD]
    values = kv_ref[:, HD:]
    d_keys = jnp.zeros((kv_ref.shape[0], HD), F32)
    d_values = jnp.zeros((kv_ref.shape[0], HD), F32)
    dqs = []
    for head in range(heads):
        cols = slice(head * HD, (head + 1) * HD)
        queries = q_ref[:, cols]
        grads = do_ref[:, cols]
        delta = jnp.sum(grads.astype(F32) * out_ref[:, cols], axis=1, keepdims=True)
        scores = dot_cols(queries, keys) + bias_ref[...]
        probs = jnp.exp(scores - lse_ref[:, head : head + 1])
        d_probs = dot_cols(grads, values)
        d_scores = (probs * (d_probs - delta)).astype(BF16)
        dqs.append(dot(d_scores, keys) * HD ** (-0.5))
        d_keys = d_keys + dot_rows(d_scores, queries)
        d_values = d_values + dot_rows(probs.astype(BF16), grads)
    dq_ref[...] = jnp.concatenate(dqs, axis=1)
    dkv_ref[...] = jnp.concatenate([d_keys, d_values], axis=1)


def per_device(
    rows,
    tokens,
    segment_ids,
    attn_gain,
    w_query,
    b_query,
    w_key,
    b_key,
    w_value,
    b_value,
    w_out,
    ffn_gain,
    w_gate,
    w_up,
    w_down,
    out_grad,
):
    count, width = tokens.shape
    half = count // 2
    d_rows = w_query.shape[0]
    q_width = w_query.shape[1]
    qk_width = q_width + HD
    lin_width = qk_width + HD
    heads = q_width // HD
    units = w_gate.shape[1] // 4
    row = lax.axis_index("row")
    group = lax.axis_index("dp")
    core = lax.axis_index("col")
    slots = dp_slots(group, core)
    first_bit = jnp.where(core == 0, 1, 2)
    second_bit = 3 - first_bit
    targets = [group, group ^ first_bit, group ^ second_bit, group ^ 3]

    def shift(step):
        return [(i, (i + step) % rows) for i in range(rows)]

    def upward(step):
        return [(i, i + step) for i in range(rows - step)]

    def downward(step):
        return [(i + step, i) for i in range(rows - step)]

    w_lin = lax.all_gather(
        jnp.concatenate([w_query, w_key, w_value], axis=1), "row", axis=0, tiled=True
    )
    w_out_t = lax.all_gather(w_out.T, "row", axis=0, tiled=True)
    own_ffn = jnp.stack(
        [
            lax.dynamic_slice_in_dim(w_gate, group * units, units, axis=1),
            lax.dynamic_slice_in_dim(w_up, group * units, units, axis=1),
            lax.dynamic_slice_in_dim(w_down, group * units, units, axis=0).T,
        ]
    )
    ffn = jnp.zeros((3, rows, d_rows, units), BF16)
    for step in range(rows):
        piece = own_ffn if step == 0 else lax.ppermute(own_ffn, "row", shift(step))
        place = (row + rows - step) % rows
        ffn = lax.dynamic_update_slice(ffn, piece[:, None], (0, place, 0, 0))
    ffn = ffn.reshape(3, width, units)
    gate_w, up_w, down_t = ffn[0], ffn[1], ffn[2]

    def split_gather(values):
        own = dp_gather(lax.dynamic_slice_in_dim(values, core * half, half, axis=0))
        own = own.reshape(4 * half, width)
        return jnp.concatenate([own, swap_core(own)], axis=0)

    def split_scatter_sum(partial):
        parts = partial.reshape(2, 4, half, width)
        kept = parts[0] + swap_core(parts[1].astype(BF16)).astype(F32)
        own = dp_scatter_sum(kept).astype(BF16)
        other = swap_core(own)
        low = jnp.where(core == 0, own, other)
        high = jnp.where(core == 0, other, own)
        return jnp.concatenate([low, high], axis=0).astype(F32)

    inputs = tokens.astype(F32)
    gain_one = attn_gain.astype(F32)[None, :]
    gain_two = ffn_gain.astype(F32)[None, :]
    inv_one = inverse_rms(inputs)
    unit_one = inputs * inv_one
    normed1 = (unit_one * gain_one).astype(BF16)
    grad_all = split_gather(out_grad)
    normed1_all = dp_gather(normed1).reshape(4 * count, width)
    bias = jnp.concatenate([b_query, b_key, b_value]).astype(F32)[None, :]
    lin = dot(normed1, w_lin) + bias
    positions = row * count + jnp.arange(count, dtype=jnp.int32)
    ladder = (jnp.arange(HD, dtype=jnp.int32) % HALF).astype(F32) * (2.0 / HD)
    angles = positions.astype(F32)[:, None] * jnp.exp(-ladder * jnp.log(ROPE_BASE))[None, :]
    cos_one, sin_one = jnp.cos(angles), jnp.sin(angles)
    cos_table = jnp.tile(cos_one, (1, heads + 1))
    sin_table = jnp.tile(sin_one, (1, heads + 1))
    qk_lin = lin[:, :qk_width]
    qk_rot = qk_lin * cos_table + half_turn(qk_lin) * sin_table
    queries = (qk_rot[:, :q_width].astype(BF16).astype(F32) * HD ** (-0.5)).astype(BF16)
    kv_own = jnp.concatenate([qk_rot[:, q_width:], lin[:, qk_width:]], axis=1).astype(BF16)
    seg_rows = count // LANES
    seg_own = jnp.zeros((EXTRA_ROWS, LANES), BF16)
    seg_own = seg_own.at[:seg_rows].set(segment_ids.astype(BF16).reshape(seg_rows, LANES))
    kv_send = jnp.concatenate([kv_own, seg_own], axis=0)
    pieces = [kv_send] + [lax.ppermute(kv_send, "row", upward(step)) for step in range(1, rows)]
    kv_all = jnp.concatenate([piece[:count] for piece in pieces], axis=0)
    key_seg = jnp.concatenate(
        [piece[count : count + seg_rows].reshape(count) for piece in pieces]
    ).astype(jnp.int32)
    block = jnp.repeat(jnp.arange(rows, dtype=jnp.int32), count)
    within = jnp.tile(jnp.arange(count, dtype=jnp.int32), rows)
    key_pos = jnp.where(block <= row, (row - block) * count + within, 2**30)
    key_meta = jnp.zeros((8, rows * count), jnp.int32).at[0].set(key_pos).at[1].set(key_seg)
    query_meta = jnp.stack([positions, segment_ids], axis=1)
    key_count = rows * count
    attend_cost = 2 * heads * count * key_count * HD
    attn_out, log_sum = pl.pallas_call(
        functools.partial(attend_kernel, heads),
        out_shape=(
            jax.ShapeDtypeStruct((count, q_width), F32),
            jax.ShapeDtypeStruct((count, LANES), F32),
        ),
        scratch_shapes=[pltpu.VMEM((count, key_count), F32)],
        compiler_params=pltpu.CompilerParams(vmem_limit_bytes=40 * 2**20),
        cost_estimate=pl.CostEstimate(
            flops=2 * attend_cost,
            bytes_accessed=2**21,
            transcendentals=heads * count * key_count,
        ),
    )(queries, kv_all, query_meta, key_meta)
    attn_heads = attn_out.astype(BF16)
    branch = dot_cols(attn_heads, w_out_t).astype(BF16)
    residual = inputs + (branch.astype(F32) + swap_core(branch).astype(F32))

    inv_two = inverse_rms(residual)
    unit_two = residual * inv_two
    normed2 = (unit_two * gain_two).astype(BF16)
    normed2_all = split_gather(normed2)
    gate_lin = dot(normed2_all, gate_w)
    up_lin = dot(normed2_all, up_w)
    d_hidden = dot(grad_all, down_t)
    sigmoid_gate = jax.nn.sigmoid(gate_lin)
    silu_gate = gate_lin * sigmoid_gate
    hidden = (silu_gate * up_lin).astype(BF16)
    d_gate = (d_hidden * up_lin * sigmoid_gate * (1.0 + gate_lin * (1.0 - sigmoid_gate))).astype(
        BF16
    )
    d_up = (d_hidden * silu_gate).astype(BF16)
    d_normed2 = split_scatter_sum(dot_cols(d_gate, gate_w) + dot_cols(d_up, up_w))
    ffn_branch = split_scatter_sum(dot_cols(hidden, down_t))
    output = (residual + ffn_branch).astype(BF16)
    ffn_grads = jnp.stack(
        [
            dot_rows(normed2_all, d_gate).astype(BF16),
            dot_rows(normed2_all, d_up).astype(BF16),
            dot_rows(grad_all, hidden).astype(BF16),
        ]
    ).reshape(3, rows, d_rows, units)

    def row_scatter(parts, axis):
        own = pick(parts, row, axis)
        others = [
            lax.ppermute(pick(parts, (row + step) % rows, axis), "row", shift(step))
            for step in range(1, rows)
        ]
        return [own] + others

    def total(parts):
        summed = parts[0].astype(F32)
        for part in parts[1:]:
            summed = summed + part.astype(F32)
        return summed

    ffn_done = dp_gather(total(row_scatter(ffn_grads, 1)).astype(BF16))

    d_res_norm, grad_gain_two = norm_back(d_normed2, unit_two, inv_two, gain_two)
    d_residual = out_grad.astype(F32) + d_res_norm
    d_residual_low = d_residual.astype(BF16)
    d_heads = dot(d_residual_low, w_out_t).astype(BF16)
    out_cols = q_width // 4
    out_part = dot_rows(d_residual_low, attn_heads).astype(BF16).reshape(width, 4, out_cols)
    out_part = jnp.stack([pick(out_part, target, 1) for target in targets])
    out_sum = dp_scatter_sum_cols(out_part)
    dq_rot, dkv_all = pl.pallas_call(
        functools.partial(attend_back_kernel, heads),
        out_shape=(
            jax.ShapeDtypeStruct((count, q_width), F32),
            jax.ShapeDtypeStruct((key_count, 2 * HD), F32),
        ),
        scratch_shapes=[pltpu.VMEM((count, key_count), F32)],
        compiler_params=pltpu.CompilerParams(vmem_limit_bytes=48 * 2**20),
        cost_estimate=pl.CostEstimate(
            flops=5 * attend_cost,
            bytes_accessed=2**22,
            transcendentals=heads * count * key_count,
        ),
    )(queries, kv_all, query_meta, key_meta, attn_out, log_sum, d_heads)
    dkv_parts = dkv_all.astype(BF16).reshape(rows, count, 2 * HD)
    dkv = total(
        [dkv_parts[0]]
        + [lax.ppermute(dkv_parts[step], "row", downward(step)) for step in range(1, rows)]
    )
    dqk_rot = jnp.concatenate([dq_rot, dkv[:, :HD]], axis=1)
    dqk = dqk_rot * cos_table - half_turn(dqk_rot) * sin_table
    d_lin = jnp.concatenate([dqk, dkv[:, HD:]], axis=1).astype(BF16)
    d_normed1 = dot_cols(d_lin, w_lin).astype(BF16)
    d_normed1 = d_normed1.astype(F32) + swap_core(d_normed1).astype(F32)
    d_in_norm, grad_gain_one = norm_back(d_normed1, unit_one, inv_one, gain_one)
    grad_tokens = (d_residual + d_in_norm).astype(BF16)

    lin_cols = lin_width // 4
    d_lin_parts = d_lin.reshape(count, 4, lin_cols)
    d_lin_parts = jnp.stack([pick(d_lin_parts, target, 1) for target in targets])
    d_lin_all = dp_exchange(d_lin_parts).reshape(4 * count, lin_cols)
    lin_sum = dot_rows(normed1_all, d_lin_all)
    bias_sum = jnp.sum(d_lin_all.astype(F32), axis=0)
    pack_width = out_cols + lin_cols
    small = jnp.concatenate([grad_gain_one, grad_gain_two, bias_sum])
    small = jnp.pad(small, (0, EXTRA_ROWS // 2 * pack_width - small.shape[0]))

    def two_halves(values):
        high = values.astype(BF16)
        low = (values - high.astype(F32)).astype(BF16)
        return jnp.concatenate([high, low]).reshape(EXTRA_ROWS, pack_width)

    small_low = two_halves(small)
    attn_grads = jnp.concatenate([out_sum, lin_sum], axis=1).astype(BF16)
    attn_grads = attn_grads.reshape(rows, d_rows, pack_width)
    attn_grads = jnp.concatenate(
        [attn_grads, jnp.broadcast_to(small_low, (rows, EXTRA_ROWS, pack_width))], axis=1
    )
    received = row_scatter(attn_grads, 0)
    attn_sum = total([piece[:d_rows] for piece in received]).astype(BF16)
    small_parts = jnp.stack([piece[d_rows:] for piece in received])
    small_sum = jnp.zeros((EXTRA_ROWS, pack_width), F32)
    for place in range(rows):
        small_sum = small_sum + pick(small_parts, (row + rows - place) % rows).astype(F32)
    small_sum = small_sum[: EXTRA_ROWS // 2] + small_sum[EXTRA_ROWS // 2 :]
    attn_done = dp_gather(jnp.concatenate([attn_sum, two_halves(small_sum.reshape(-1))], axis=0))

    ffn_pieces = [pick(ffn_done, slot) for slot in slots]
    attn_pieces = [pick(attn_done, slot) for slot in slots]

    def joined(parts):
        return jnp.concatenate(parts, axis=1).astype(F32)

    grad_w_gate = joined([piece[0] for piece in ffn_pieces])
    grad_w_up = joined([piece[1] for piece in ffn_pieces])
    grad_w_down = joined([piece[2] for piece in ffn_pieces]).T
    grad_w_out = joined([piece[:d_rows, :out_cols] for piece in attn_pieces]).T
    grad_w_lin = joined([piece[:d_rows, out_cols:] for piece in attn_pieces])
    smalls = [
        piece[d_rows : d_rows + EXTRA_ROWS // 2].astype(F32).reshape(-1)
        + piece[d_rows + EXTRA_ROWS // 2 :].astype(F32).reshape(-1)
        for piece in attn_pieces
    ]
    gains = total([small_piece[: 2 * width] for small_piece in smalls])
    biases = jnp.concatenate(
        [small_piece[2 * width : 2 * width + lin_cols] for small_piece in smalls]
    )
    return (
        output,
        grad_tokens,
        gains[:width],
        grad_w_lin[:, :q_width],
        biases[:q_width],
        grad_w_lin[:, q_width:qk_width],
        biases[q_width:qk_width],
        grad_w_lin[:, qk_width:],
        biases[qk_width:],
        grad_w_out,
        gains[width:],
        grad_w_gate,
        grad_w_up,
        grad_w_down,
    )


def solution(mesh):
    return jax.shard_map(
        functools.partial(per_device, mesh.shape["row"]),
        mesh=mesh,
        in_specs=(
            P(("dp", "row"), None),
            P(("dp", "row")),
            P(),
            P("row", "col"),
            P("col"),
            P("row", "col"),
            P("col"),
            P("row", "col"),
            P("col"),
            P("col", "row"),
            P(),
            P("row", "col"),
            P("row", "col"),
            P("col", "row"),
            P(("dp", "row"), None),
        ),
        out_specs=(
            P(("dp", "row"), None),
            P(("dp", "row"), None),
            P(),
            P("row", "col"),
            P("col"),
            P("row", "col"),
            P("col"),
            P("row", "col"),
            P("col"),
            P("col", "row"),
            P(),
            P("row", "col"),
            P("row", "col"),
            P("col", "row"),
        ),
        check_vma=False,
    )
```

time: 938 us -> 423 us (0.45)
  waiting for transfers between devices: 538 us -> 134 us
  blocking collectives: 213 us -> 97.9 us
  matrix products: 81.8 us -> 30.7 us
  starting transfers between devices: 20.6 us -> 47.6 us
  local copies, waits for them, and re-layouts: 33.5 us -> 55.7 us
  between operations: 16.1 us -> 2.47 us
  Pallas kernels: 0 us -> 9.9 us
    all_gather x6 -> x0, waiting for transfers between devices: 413 us -> none  [the longest x1 171 us: per_device(): lax.all_gather(ffn_grad, 'row', axis=0, tiled=True)]
    ppermute x0 -> x41, waiting for transfers between devices: none -> 134 us  [the longest x6 69.5 us: row_scatter(): lax.ppermute(pick(parts, (row + step) % rows, axis), 'row', shift(step))]
    psum x1 -> x0, blocking collectives: 75.2 us -> none  [per_device(): lax.psum((jnp.sum(d_query, axis=0, dtype=jnp.float32), jnp.sum(d_key, axi...]
    all_to_all x4 -> x0, waiting for transfers between devices: 54.4 us -> none  [the longest x1 21.7 us: per_device(): lax.all_to_all(d_residual_low, 'row', split_axis=1, concat_axis=0, tiled=...]
    dot_general x32 -> x15, matrix products: 81.8 us -> 30.7 us  [the longest x5 14.4 us: dot_rows(): lax.dot_general(left, right, (((0,), (0,)), ((), ())), preferred_element_...]
    psum x4 -> x0, waiting for transfers between devices: 49.8 us -> none  [the longest x1 17.1 us: per_device(): lax.psum(shortened(partial_grads), 'dp')]
    ppermute x0 -> x41, starting transfers between devices: none -> 47.6 us  [the longest x18 20.8 us: dp_step(): return lax.ppermute(value, ('dp', 'col'), pairs)]
    all_gather x7 -> x2, blocking collectives: 138 us -> 97.9 us  [the longest x1 72.7 us: per_device(): w_out_t = lax.all_gather(w_out.T, 'row', axis=0, tiled=True)]
  transfers between devices with their start and end apart: 15 -> 41, of which waited for: 12 -> 17; matrix products, arithmetic and copies ran while one was open for 6% -> 21% of each run, Pallas kernels for 0% -> 2%
where the time goes in v1:
time: 423 us; the launch traced here: 417 us
  waiting for transfers between devices  134 us (32%)
  blocking collectives  97.9 us (23%)
  local copies, waits for them, and re-layouts  55.7 us (13%)
  starting transfers between devices  47.6 us (11%)
  other arithmetic  38.9 us (9%)
  matrix products  30.7 us (7%)
  Pallas kernels  9.9 us (2%)
    all_gather x1, blocking collectives, per_device(): w_out_t = lax.all_gather(w_out.T, 'row', axis=0, tiled=True)  72.7 us
    ppermute x6, waiting for transfers between devices, row_scatter(): lax.ppermute(pick(parts, (row + step) % rows, axis), 'row', shift(step))  69.5 us
    ppermute x18, waiting for transfers between devices, dp_step(): return lax.ppermute(value, ('dp', 'col'), pairs)  59.5 us
    all_gather x1, blocking collectives, per_device(): lax.all_gather(jnp.concatenate([w_query, w_key, w_value], axis=1), 'row',...  25.3 us
    ppermute x18, starting transfers between devices, dp_step(): return lax.ppermute(value, ('dp', 'col'), pairs)  20.8 us
    dot_general x5, matrix products, dot_rows(): lax.dot_general(left, right, (((0,), (0,)), ((), ())), preferred_element_...  14.4 us
    unnamed x129, local copies, waits for them, and re-layouts  13.7 us
    ppermute x3, starting transfers between devices, per_device(): lax.ppermute(kv_send, 'row', upward(step))  9.98 us
  transfers between devices with their start and end apart: 41, of which 17 were waited for; matrix products, arithmetic and copies ran while one was open for 21% of the time, Pallas kernels for 2%

profile of v1, /device:TPU:0, one launch (start us, length us, event | category | flops | bytes accessed | tf_op | source)
XLA Modules:
  0.0 417.2 jit_solution(7983914307609627588)
XLA Ops:
  5.5 25.3 %all_gather.6 = bf16[896,576]{1,0:T(8,128)(2,1)S(1)} all-gather(bf16[224,576]{1,0:T(8,128)(2,1)S(1)} %pad_maximum_fusion.19), channel_id=1, replica_groups=mesh['dp'=4,'row'=4,'col'=2] {'row'}, dimensions={0}, use_global_device_ids=true | all-gather | bytes 1290240 | tf_op jit(solution)/shard_map/all_gather | solution.py:193
  32.0 1.6 convolution_add_fusion.1
  38.9 1.8 fusion.41
  41.0 5.6 %collective-permute-start.2 = (bf16[272,128]{1,0:T(8,128)(2,1)S(1)}, bf16[272,128]{1,0:T(8,128)(2,1)}, u32[]{:S(2)}, u32[]{:S(2)}) collective-permute-start(bf16[272,128]{1,0:T(8,128)(2,1)S(1)} %fusion.64), channel_id=1, source_target_pairs={{0,6},{1,7},{8,14},{9,15},{16,22},{17,23},{24,30},{25,31}} | collective-permute-start | bytes 208904 | tf_op jit(solution)/shard_map/ppermute | solution.py:250
  46.6 1.9 collective-permute-start.1
  48.5 2.5 collective-permute-start
  51.1 1.5 dynamic-slice_bitcast_fusion.16
  54.0 72.7 %all_gather.7 = bf16[896,448]{1,0:T(8,128)(2,1)S(1)} all-gather(bf16[224,448]{1,0:T(8,128)(2,1)S(1)} %bitcast.249), channel_id=1, replica_groups=mesh['dp'=4,'row'=4,'col'=2] {'row'}, dimensions={0}, use_global_device_ids=true | all-gather | bytes 1003520 | tf_op jit(solution)/shard_map/all_gather | solution.py:196
  126.9 4.1 collective-permute-start.9
  136.3 3.8 shard_map.254
  141.5 1.5 collective-permute-start.14
  145.3 2.5 collective-permute-done.14
  147.8 1.6 collective-permute-start.15
  152.9 6.0 %collective-permute-done.15 = bf16[2,128,896]{2,1,0:T(8,128)(2,1)S(1)} collective-permute-done((bf16[2,128,896]{2,1,0:T(8,128)(2,1)S(1)}, bf16[2,128,896]{2,1,0:T(8,128)(2,1)S(1)}, u32[]{:S(2)}, u32[]{:S(2)}) %collective-permute-start.15) | collective-permute-done | bytes 458784 | tf_op jit(solution)/shard_map/ppermute | solution.py:53
  159.0 1.7 collective-permute-start.27
  165.6 4.8 %collective-permute-done.5 = bf16[2,128,896]{2,1,0:T(8,128)(2,1)S(1)} collective-permute-done((bf16[2,128,896]{2,1,0:T(8,128)(2,1)S(1)}, bf16[2,128,896]{2,1,0:T(8,128)(2,1)S(1)}, u32[]{:S(2)}, u32[]{:S(2)}) %collective-permute-start.5) | collective-permute-done | bytes 458784 | tf_op jit(solution)/shard_map/ppermute | solution.py:53
  170.6 2.0 collective-permute-start.6
  174.2 1.5 fusion.20
  175.8 1.5 fusion.81
  177.3 3.9 multiply_convert_fusion.1
  181.2 1.8 fusion.92
  183.1 1.8 convolution_add_fusion
  184.9 1.8 copy-done.2
  188.0 2.5 convolution_convert_fusion
  190.6 2.4 copy.113
  192.9 4.4 %convolution_convert_fusion.1 = bf16[896,608]{0,1:T(8,128)(2,1)} fusion(bf16[1024,608]{0,1:T(8,128)(2,1)} %copy-done.55, bf16[512,896]{1,0:T(8,128)(2,1)} %copy-done.52, bf16[512,896]{1,0:T(8,128)(2,1)} %bitcast.245), kind=kOutput, calls=%fused_computation.27 | convolution fusion | flops 1119899648 | bytes 4169728 | tf_op jit(solution)/shard_map/dot_general | solution.py:22
  197.3 2.4 copy.112
  199.7 4.4 %convolution_convert_fusion.2 = bf16[896,608]{0,1:T(8,128)(2,1)} fusion(bf16[1024,608]{0,1:T(8,128)(2,1)} %copy-done.18, bf16[512,896]{1,0:T(8,128)(2,1)} %copy-done.52, bf16[512,896]{1,0:T(8,128)(2,1)} %bitcast.246), kind=kOutput, calls=%fused_computation.28 | convolution fusion | flops 1119899648 | bytes 4169728 | tf_op jit(solution)/shard_map/dot_general | solution.py:22
  204.0 2.4 copy.111
  206.4 2.2 pad_maximum_fusion
  209.1 2.1 collective-permute-start.36
  211.2 1.8 fusion.91
  214.5 2.0 pad_maximum_fusion.9
  219.5 12.0 %collective-permute-done.38 = bf16[3,224,608]{2,1,0:T(8,128)(2,1)S(1)} collective-permute-done((bf16[3,224,608]{2,1,0:T(8,128)(2,1)S(1)}, bf16[3,224,608]{2,1,0:T(8,128)(2,1)S(1)}, u32[]{:S(2)}, u32[]{:S(2)}) %collective-permute-start.38) | collective-permute-done | bytes 817184 | tf_op jit(solution)/shard_map/ppermute | solution.py:308
  232.8 50.0 %collective-permute-done.37 = bf16[3,224,608]{2,1,0:T(8,128)(2,1)S(1)} collective-permute-done((bf16[3,224,608]{2,1,0:T(8,128)(2,1)S(1)}, bf16[3,224,608]{2,1,0:T(8,128)(2,1)S(1)}, u32[]{:S(2)}, u32[]{:S(2)}) %collective-permute-start.37) | collective-permute-done | bytes 817184 | tf_op jit(solution)/shard_map/ppermute | solution.py:308
  283.3 1.6 collective-permute-start.39
  285.1 1.5 collective-permute-start.11
  287.4 11.3 %collective-permute-done.11 = bf16[2,128,896]{2,1,0:T(8,128)(2,1)S(1)} collective-permute-done((bf16[2,128,896]{2,1,0:T(8,128)(2,1)S(1)}, bf16[2,128,896]{2,1,0:T(8,128)(2,1)S(1)}, u32[]{:S(2)}, u32[]{:S(2)}) %collective-permute-start.11) | collective-permute-done | bytes 458784 | tf_op jit(solution)/shard_map/ppermute | solution.py:53
  299.3 4.1 collective-permute-done.19
  303.6 2.3 collective-permute-done.12
  312.9 6.1 %shard_map.255 = (f32[256,448]{1,0:T(8,128)S(1)}, f32[1024,128]{1,0:T(8,128)S(1)}) custom-call(bf16[256,448]{1,0:T(8,128)(2,1)S(1)} %multiply_convert_fusion.3.q_ref, bf16[1024,128]{1,0:T(8,128)(2,1)S(1)} %pad_maximum_fusion.20.kv_ref, s32[256,2]{1,0:T(8,128)S(1)} %copy.102.qm_ref, s32[8,1024]{1,0:T(8,128)S(1)} %scatter.14.km_ref, ...), custom_call_target="tpu_custom_call" | custom-call | flops 1174405120 | bytes 4194304 | tf_op jit(solution)/shard_map/pallas_call | solution.py:329
  321.6 1.5 collective-permute-start.21
  324.6 2.8 collective-permute-done.23
  327.8 2.3 collective-permute-done.22
  333.6 1.5 collective-permute-start.29
  336.7 3.7 collective-permute-done.29
  341.8 15.2 %collective-permute-done.30 = bf16[2,256,144]{1,2,0:T(8,128)(2,1)S(1)} collective-permute-done((bf16[2,256,144]{1,2,0:T(8,128)(2,1)S(1)}, bf16[2,256,144]{1,2,0:T(8,128)(2,1)S(1)}, u32[]{:S(2)}, u32[]{:S(2)}) %collective-permute-start.30) | collective-permute-done | bytes 147488 | tf_op jit(solution)/shard_map/ppermute | solution.py:53
  357.7 1.8 fusion.17
  364.1 1.5 fusion.33
  365.6 3.7 collective-permute-done.26
  372.5 3.0 collective-permute-start.33
  377.3 2.0 collective-permute-done.33
  379.2 5.5 %collective-permute-done.32 = bf16[240,256]{1,0:T(8,128)(2,1)S(1)} collective-permute-done((bf16[240,256]{1,0:T(8,128)(2,1)S(1)}, bf16[240,256]{1,0:T(8,128)(2,1)S(1)}, u32[]{:S(2)}, u32[]{:S(2)}) %collective-permute-start.32) | collective-permute-done | bytes 122912 | tf_op jit(solution)/shard_map/ppermute | solution.py:308
  384.9 1.8 collective-permute-start.34
  386.7 3.2 collective-permute-done.34
  391.1 2.5 fusion.32
  393.6 2.6 collective-permute-done.35
  402.5 1.8 pad_maximum_fusion.1
  405.6 2.7 concatenate.183
  408.3 1.5 convert_element_type.416
  409.8 2.4 concatenate.184
  412.2 1.5 convert_element_type.417
  413.7 1.7 concatenate.185
  415.4 1.5 convert_bitcast_fusion
  (332 shorter events, 78.4 us)
Async XLA Ops:
  0.6 50.3 %copy-start = (bf16[2432,224]{0,1:T(8,128)(2,1)S(1)}, bf16[2432,224]{0,1:T(8,128)(2,1)}, u32[]{:S(2)}) copy-start(bf16[2432,224]{0,1:T(8,128)(2,1)} %param.34) | copy-start | bytes 3268612
  0.7 30.1 %copy-start.3 = (bf16[256,896]{1,0:T(8,128)(2,1)S(1)}, bf16[256,896]{1,0:T(8,128)(2,1)}, u32[]{:S(2)}) copy-start(bf16[256,896]{1,0:T(8,128)(2,1)} %param.21) | copy-start | bytes 1376260
  0.7 31.3 %copy-start.50 = (bf16[64]{0:T(256)(128)(2,1)S(1)}, bf16[64]{0:T(256)(128)(2,1)}, u32[]{:S(2)}) copy-start(bf16[64]{0:T(256)(128)(2,1)} %param.29) | copy-start | bytes 388
  0.7 31.3 %copy-start.51 = (bf16[64]{0:T(256)(128)(2,1)S(1)}, bf16[64]{0:T(256)(128)(2,1)}, u32[]{:S(2)}) copy-start(bf16[64]{0:T(256)(128)(2,1)} %param.27) | copy-start | bytes 388
  0.7 31.3 %copy-start.48 = (bf16[448]{0:T(512)(128)(2,1)S(1)}, bf16[448]{0:T(512)(128)(2,1)}, u32[]{:S(2)}) copy-start(bf16[448]{0:T(512)(128)(2,1)} %param.25) | copy-start | bytes 2692
  38.9 12.2 %copy-start.12 = (f32[256,512]{1,0:T(8,128)}, f32[256,512]{1,0:T(8,128)S(1)}, u32[]{:S(2)}) copy-start(f32[256,512]{1,0:T(8,128)S(1)} %copy.101) | copy-start | bytes 1572868
  40.9 10.1 %copy-start.42 = (bf16[256,64]{1,0:T(8,128)(2,1)}, bf16[256,64]{1,0:T(8,128)(2,1)S(1)}, u32[]{:S(2)}) copy-start(bf16[256,64]{1,0:T(8,128)(2,1)S(1)} %slice.526) | copy-start | bytes 98308
  41.0 85.9 %collective-permute-start.2 = (bf16[272,128]{1,0:T(8,128)(2,1)S(1)}, bf16[272,128]{1,0:T(8,128)(2,1)}, u32[]{:S(2)}, u32[]{:S(2)}) collective-permute-start(bf16[272,128]{1,0:T(8,128)(2,1)S(1)} %fusion.64), channel_id=1, source_target_pairs={{0,6},{1,7},{8,14},{9,15},{16,22},{17,23},{24,30},{25,31}} | collective-permute-start | bytes 208904 | tf_op jit(solution)/shard_map/ppermute | solution.py:250
  46.6 85.1 %collective-permute-start.1 = (bf16[272,128]{1,0:T(8,128)(2,1)S(1)}, bf16[272,128]{1,0:T(8,128)(2,1)}, u32[]{:S(2)}, u32[]{:S(2)}) collective-permute-start(bf16[272,128]{1,0:T(8,128)(2,1)S(1)} %fusion.64), channel_id=1, source_target_pairs={{0,4},{2,6},{1,5},{3,7},{8,12},{10,14},{9,13},{11,15},{16,20},{18,... | collective-permute-start | bytes 208904 | tf_op jit(solution)/shard_map/ppermute | solution.py:250
  48.5 83.9 %collective-permute-start = (bf16[272,128]{1,0:T(8,128)(2,1)S(1)}, bf16[272,128]{1,0:T(8,128)(2,1)}, u32[]{:S(2)}, u32[]{:S(2)}) collective-permute-start(bf16[272,128]{1,0:T(8,128)(2,1)S(1)} %fusion.64), channel_id=1, source_target_pairs={{0,2},{2,4},{4,6},{1,3},{3,5},{5,7},{8,10},{10,12},{12,14},{9,11},... | collective-permute-start | bytes 208904 | tf_op jit(solution)/shard_map/ppermute | solution.py:250
  52.7 82.9 %copy-start.41 = (bf16[256,64]{1,0:T(8,128)(2,1)S(1)}, bf16[256,64]{1,0:T(8,128)(2,1)}, u32[]{:S(2)}) copy-start(bf16[256,64]{1,0:T(8,128)(2,1)} %slice.673) | copy-start | bytes 98308
  52.7 82.9 %copy-start.43 = (bf16[256,64]{1,0:T(8,128)(2,1)S(1)}, bf16[256,64]{1,0:T(8,128)(2,1)}, u32[]{:S(2)}) copy-start(bf16[256,64]{1,0:T(8,128)(2,1)} %copy-done.42) | copy-start | bytes 98308
  53.7 108.1 %collective-permute-start.7 = (bf16[3,224,608]{2,1,0:T(8,128)(2,1)}, bf16[3,224,608]{2,1,0:T(8,128)(2,1)}, u32[]{:S(2)}, u32[]{:S(2)}) collective-permute-start(bf16[3,224,608]{2,1,0:T(8,128)(2,1)} %pad_maximum_fusion.10), channel_id=1, source_target_pairs={{0,2},{2,4},{4,6},{6,0},{1,3},{3,5},{5,7},{7,1},{8,10},{10,12},{12... | collective-permute-start | bytes 2451464 | tf_op jit(solution)/shard_map/ppermute | solution.py:206
  53.7 110.6 %collective-permute-start.8 = (bf16[3,224,608]{2,1,0:T(8,128)(2,1)}, bf16[3,224,608]{2,1,0:T(8,128)(2,1)}, u32[]{:S(2)}, u32[]{:S(2)}) collective-permute-start(bf16[3,224,608]{2,1,0:T(8,128)(2,1)} %pad_maximum_fusion.10), channel_id=1, source_target_pairs={{0,4},{2,6},{4,0},{6,2},{1,5},{3,7},{5,1},{7,3},{8,12},{10,14},{12... | collective-permute-start | bytes 2451464 | tf_op jit(solution)/shard_map/ppermute | solution.py:206
  126.6 13.6 %copy-start.5 = (bf16[896,448]{1,0:T(8,128)(2,1)}, bf16[896,448]{1,0:T(8,128)(2,1)S(1)}, u32[]{:S(2)}) copy-start(bf16[896,448]{1,0:T(8,128)(2,1)S(1)} %all_gather.7) | copy-start | bytes 2408452
  126.9 45.7 %collective-permute-start.9 = (bf16[3,224,608]{2,1,0:T(8,128)(2,1)}, bf16[3,224,608]{2,1,0:T(8,128)(2,1)}, u32[]{:S(2)}, u32[]{:S(2)}) collective-permute-start(bf16[3,224,608]{2,1,0:T(8,128)(2,1)} %pad_maximum_fusion.10), channel_id=1, source_target_pairs={{0,6},{2,0},{4,2},{6,4},{1,7},{3,1},{5,3},{7,5},{8,14},{10,8},{12,... | collective-permute-start | bytes 2451464 | tf_op jit(solution)/shard_map/ppermute | solution.py:206
  140.7 8.7 %collective-permute-start.3 = (bf16[256,896]{1,0:T(8,128)(2,1)S(1)}, bf16[256,896]{1,0:T(8,128)(2,1)S(1)}, u32[]{:S(2)}, u32[]{:S(2)}) collective-permute-start(bf16[256,896]{1,0:T(8,128)(2,1)S(1)} %convolution_convert_fusion.4), channel_id=1, source_target_pairs={{0,1},{1,0},{2,3},{3,2},{4,5},{5,4},{6,7},{7,6},{8,9},{9,8},{10,11... | collective-permute-start | bytes 1376264 | tf_op jit(solution)/shard_map/ppermute | solution.py:44
  141.5 6.2 %collective-permute-start.14 = (bf16[128,896]{1,0:T(8,128)(2,1)}, bf16[128,896]{1,0:T(8,128)(2,1)S(1)}, u32[]{:S(2)}, u32[]{:S(2)}) collective-permute-start(bf16[128,896]{1,0:T(8,128)(2,1)} %constant_dynamic-slice_fusion.13), channel_id=1, source_target_pairs={{0,8},{1,17},{8,0},{9,25},{16,24},{17,1},{24,16},{25,9},{2,10},{3,... | collective-permute-start | bytes 688136 | tf_op jit(solution)/shard_map/ppermute | solution.py:53
  147.8 11.2 %collective-permute-start.15 = (bf16[2,128,896]{2,1,0:T(8,128)(2,1)S(1)}, bf16[2,128,896]{2,1,0:T(8,128)(2,1)S(1)}, u32[]{:S(2)}, u32[]{:S(2)}) collective-permute-start(bf16[2,128,896]{2,1,0:T(8,128)(2,1)S(1)} %pad_maximum_fusion.16), channel_id=1, source_target_pairs={{0,16},{1,9},{8,24},{9,1},{16,0},{17,25},{24,8},{25,17},{2,18},{3,... | collective-permute-start | bytes 1376264 | tf_op jit(solution)/shard_map/ppermute | solution.py:53
  151.4 156.8 %copy-start.4 = (f32[256,896]{1,0:T(8,128)}, f32[256,896]{1,0:T(8,128)S(1)}, u32[]{:S(2)}) copy-start(f32[256,896]{1,0:T(8,128)S(1)} %broadcast_multiply_fusion) | copy-start | bytes 2752516
  151.4 10.3 %collective-permute-start.4 = (bf16[128,896]{1,0:T(8,128)(2,1)S(1)}, bf16[128,896]{1,0:T(8,128)(2,1)S(1)}, u32[]{:S(2)}, u32[]{:S(2)}) collective-permute-start(bf16[128,896]{1,0:T(8,128)(2,1)S(1)} %fusion.50), channel_id=1, source_target_pairs={{0,8},{1,17},{8,0},{9,25},{16,24},{17,1},{24,16},{25,9},{2,10},{3,... | collective-permute-start | bytes 688136 | tf_op jit(solution)/shard_map/ppermute | solution.py:53
  159.0 54.2 %collective-permute-start.27 = (bf16[256,896]{1,0:T(8,128)(2,1)}, bf16[256,896]{1,0:T(8,128)(2,1)}, u32[]{:S(2)}, u32[]{:S(2)}) collective-permute-start(bf16[256,896]{1,0:T(8,128)(2,1)} %fusion.27), channel_id=1, source_target_pairs={{0,8},{1,17},{8,0},{9,25},{16,24},{17,1},{24,16},{25,9},{2,10},{3,... | collective-permute-start | bytes 1376264 | tf_op jit(solution)/shard_map/ppermute | solution.py:53
  161.7 12.5 %collective-permute-start.16 = (bf16[512,896]{1,0:T(8,128)(2,1)S(1)}, bf16[512,896]{1,0:T(8,128)(2,1)S(1)}, u32[]{:S(2)}, u32[]{:S(2)}) collective-permute-start(bf16[512,896]{1,0:T(8,128)(2,1)S(1)} %bitcast.239), channel_id=1, source_target_pairs={{0,1},{1,0},{2,3},{3,2},{4,5},{5,4},{6,7},{7,6},{8,9},{9,8},{10,11... | collective-permute-start | bytes 2752520 | tf_op jit(solution)/shard_map/ppermute | solution.py:44
  161.9 8.5 %collective-permute-start.5 = (bf16[2,128,896]{2,1,0:T(8,128)(2,1)S(1)}, bf16[2,128,896]{2,1,0:T(8,128)(2,1)S(1)}, u32[]{:S(2)}, u32[]{:S(2)}) collective-permute-start(bf16[2,128,896]{2,1,0:T(8,128)(2,1)S(1)} %pad_maximum_fusion.15), channel_id=1, source_target_pairs={{0,16},{1,9},{8,24},{9,1},{16,0},{17,25},{24,8},{25,17},{2,18},{3,... | collective-permute-start | bytes 1376264 | tf_op jit(solution)/shard_map/ppermute | solution.py:53
  170.5 6.8 %copy-start.39 = (bf16[4,128,896]{2,1,0:T(8,128)(2,1)}, bf16[4,128,896]{2,1,0:T(8,128)(2,1)S(1)}, u32[]{:S(2)}) copy-start(bf16[4,128,896]{2,1,0:T(8,128)(2,1)S(1)} %pad_maximum_fusion.7) | copy-start | bytes 2752516
  170.6 5.2 %collective-permute-start.6 = (bf16[512,896]{1,0:T(8,128)(2,1)S(1)}, bf16[512,896]{1,0:T(8,128)(2,1)S(1)}, u32[]{:S(2)}, u32[]{:S(2)}) collective-permute-start(bf16[512,896]{1,0:T(8,128)(2,1)S(1)} %bitcast.242), channel_id=1, source_target_pairs={{0,1},{1,0},{2,3},{3,2},{4,5},{5,4},{6,7},{7,6},{8,9},{9,8},{10,11... | collective-permute-start | bytes 2752520 | tf_op jit(solution)/shard_map/ppermute | solution.py:44
  181.2 6.8 %copy-start.53 = (bf16[1024,608]{0,1:T(8,128)(2,1)}, bf16[1024,608]{0,1:T(8,128)(2,1)S(1)}, u32[]{:S(2)}) copy-start(bf16[1024,608]{0,1:T(8,128)(2,1)S(1)} %get-tuple-element.136) | copy-start | bytes 3735556
  187.8 28.8 %collective-permute-start.17 = (bf16[4,128,896]{2,1,0:T(8,128)(2,1)}, bf16[4,128,896]{2,1,0:T(8,128)(2,1)}, u32[]{:S(2)}, u32[]{:S(2)}) collective-permute-start(bf16[4,128,896]{2,1,0:T(8,128)(2,1)} %bitcast.27), channel_id=1, source_target_pairs={{0,1},{1,0},{2,3},{3,2},{4,5},{5,4},{6,7},{7,6},{8,9},{9,8},{10,11... | collective-permute-start | bytes 2752520 | tf_op jit(solution)/shard_map/ppermute | solution.py:44
  209.0 22.5 %collective-permute-start.38 = (bf16[3,224,608]{2,1,0:T(8,128)(2,1)S(1)}, bf16[3,224,608]{2,1,0:T(8,128)(2,1)S(1)}, u32[]{:S(2)}, u32[]{:S(2)}) collective-permute-start(bf16[3,224,608]{2,1,0:T(8,128)(2,1)S(1)} %get-tuple-element.150), channel_id=1, source_target_pairs={{0,6},{2,0},{4,2},{6,4},{1,7},{3,1},{5,3},{7,5},{8,14},{10,8},{12,... | collective-permute-start | bytes 2451464 | tf_op jit(solution)/shard_map/ppermute | solution.py:308
  209.0 73.8 %collective-permute-start.37 = (bf16[3,224,608]{2,1,0:T(8,128)(2,1)S(1)}, bf16[3,224,608]{2,1,0:T(8,128)(2,1)S(1)}, u32[]{:S(2)}, u32[]{:S(2)}) collective-permute-start(bf16[3,224,608]{2,1,0:T(8,128)(2,1)S(1)} %get-tuple-element.151), channel_id=1, source_target_pairs={{0,4},{2,6},{4,0},{6,2},{1,5},{3,7},{5,1},{7,3},{8,12},{10,14},{12... | collective-permute-start | bytes 2451464 | tf_op jit(solution)/shard_map/ppermute | solution.py:308
  209.1 73.7 %collective-permute-start.36 = (bf16[3,224,608]{2,1,0:T(8,128)(2,1)S(1)}, bf16[3,224,608]{2,1,0:T(8,128)(2,1)S(1)}, u32[]{:S(2)}, u32[]{:S(2)}) collective-permute-start(bf16[3,224,608]{2,1,0:T(8,128)(2,1)S(1)} %get-tuple-element.149), channel_id=1, source_target_pairs={{0,2},{2,4},{4,6},{6,0},{1,3},{3,5},{5,7},{7,1},{8,10},{10,12},{12... | collective-permute-start | bytes 2451464 | tf_op jit(solution)/shard_map/ppermute | solution.py:308
  213.2 71.7 %collective-permute-start.10 = (bf16[4,128,896]{2,1,0:T(8,128)(2,1)S(1)}, bf16[4,128,896]{2,1,0:T(8,128)(2,1)S(1)}, u32[]{:S(2)}, u32[]{:S(2)}) collective-permute-start(bf16[4,128,896]{2,1,0:T(8,128)(2,1)S(1)} %bitcast.247), channel_id=1, source_target_pairs={{0,1},{1,0},{2,3},{3,2},{4,5},{5,4},{6,7},{7,6},{8,9},{9,8},{10,11... | collective-permute-start | bytes 2752520 | tf_op jit(solution)/shard_map/ppermute | solution.py:44
  216.6 125.2 %collective-permute-start.28 = (bf16[2,256,896]{2,1,0:T(8,128)(2,1)}, bf16[2,256,896]{2,1,0:T(8,128)(2,1)}, u32[]{:S(2)}, u32[]{:S(2)}) collective-permute-start(bf16[2,256,896]{2,1,0:T(8,128)(2,1)} %pad_maximum_fusion.9), channel_id=1, source_target_pairs={{0,16},{1,9},{8,24},{9,1},{16,0},{17,25},{24,8},{25,17},{2,18},{3,... | collective-permute-start | bytes 2752520 | tf_op jit(solution)/shard_map/ppermute | solution.py:53
  219.5 65.4 %slice-start.1 = ((f32[1024,896]{1,0:T(8,128)}), f32[512,896]{1,0:T(8,128)S(1)}, s32[]{:S(2)}) async-start(f32[1024,896]{1,0:T(8,128)} %copy-done.9), calls=%async_computation.1 | async-start | bytes 3670016 | tf_op jit(solution)/shard_map/slice | solution.py:219
  231.5 55.1 %collective-permute-start.18 = (bf16[2,128,896]{2,1,0:T(8,128)(2,1)S(1)}, bf16[2,128,896]{2,1,0:T(8,128)(2,1)S(1)}, u32[]{:S(2)}, u32[]{:S(2)}) collective-permute-start(bf16[2,128,896]{2,1,0:T(8,128)(2,1)S(1)} %slice.671), channel_id=1, source_target_pairs={{0,16},{1,9},{8,24},{9,1},{16,0},{17,25},{24,8},{25,17},{2,18},{3,... | collective-permute-start | bytes 1376264 | tf_op jit(solution)/shard_map/ppermute | solution.py:53
  283.3 23.4 %copy-start.7 = (bf16[3,224,608]{2,1,0:T(8,128)(2,1)}, bf16[3,224,608]{2,1,0:T(8,128)(2,1)S(1)}, u32[]{:S(2)}) copy-start(bf16[3,224,608]{2,1,0:T(8,128)(2,1)S(1)} %fusion.9) | copy-start | bytes 2451460
  283.3 23.4 %collective-permute-start.39 = (bf16[3,224,608]{2,1,0:T(8,128)(2,1)S(1)}, bf16[3,224,608]{2,1,0:T(8,128)(2,1)S(1)}, u32[]{:S(2)}, u32[]{:S(2)}) collective-permute-start(bf16[3,224,608]{2,1,0:T(8,128)(2,1)S(1)} %fusion.9), channel_id=1, source_target_pairs={{0,8},{1,17},{8,0},{9,25},{16,24},{17,1},{24,16},{25,9},{2,10},{3,... | collective-permute-start | bytes 2451464 | tf_op jit(solution)/shard_map/ppermute | solution.py:53
  285.1 13.5 %collective-permute-start.11 = (bf16[2,128,896]{2,1,0:T(8,128)(2,1)S(1)}, bf16[2,128,896]{2,1,0:T(8,128)(2,1)S(1)}, u32[]{:S(2)}, u32[]{:S(2)}) collective-permute-start(bf16[2,128,896]{2,1,0:T(8,128)(2,1)S(1)} %slice.672), channel_id=1, source_target_pairs={{0,16},{1,9},{8,24},{9,1},{16,0},{17,25},{24,8},{25,17},{2,18},{3,... | collective-permute-start | bytes 1376264 | tf_op jit(solution)/shard_map/ppermute | solution.py:53
  286.7 16.7 %collective-permute-start.19 = (bf16[128,896]{1,0:T(8,128)(2,1)S(1)}, bf16[128,896]{1,0:T(8,128)(2,1)S(1)}, u32[]{:S(2)}, u32[]{:S(2)}) collective-permute-start(bf16[128,896]{1,0:T(8,128)(2,1)S(1)} %fusion.54), channel_id=1, source_target_pairs={{0,8},{1,17},{8,0},{9,25},{16,24},{17,1},{24,16},{25,9},{2,10},{3,... | collective-permute-start | bytes 688136 | tf_op jit(solution)/shard_map/ppermute | solution.py:53
  298.8 7.1 %collective-permute-start.12 = (bf16[128,896]{1,0:T(8,128)(2,1)S(1)}, bf16[128,896]{1,0:T(8,128)(2,1)S(1)}, u32[]{:S(2)}, u32[]{:S(2)}) collective-permute-start(bf16[128,896]{1,0:T(8,128)(2,1)S(1)} %fusion.53), channel_id=1, source_target_pairs={{0,8},{1,17},{8,0},{9,25},{16,24},{17,1},{24,16},{25,9},{2,10},{3,... | collective-permute-start | bytes 688136 | tf_op jit(solution)/shard_map/ppermute | solution.py:53
  303.5 4.6 %collective-permute-start.20 = (bf16[128,896]{1,0:T(8,128)(2,1)S(1)}, bf16[128,896]{1,0:T(8,128)(2,1)S(1)}, u32[]{:S(2)}, u32[]{:S(2)}) collective-permute-start(bf16[128,896]{1,0:T(8,128)(2,1)S(1)} %fusion.47), channel_id=1, source_target_pairs={{0,1},{1,0},{2,3},{3,2},{4,5},{5,4},{6,7},{7,6},{8,9},{9,8},{10,11... | collective-permute-start | bytes 688136 | tf_op jit(solution)/shard_map/ppermute | solution.py:44
  306.7 68.8 %collective-permute-start.13 = (bf16[128,896]{1,0:T(8,128)(2,1)}, bf16[128,896]{1,0:T(8,128)(2,1)}, u32[]{:S(2)}, u32[]{:S(2)}) collective-permute-start(bf16[128,896]{1,0:T(8,128)(2,1)} %fusion.49), channel_id=1, source_target_pairs={{0,1},{1,0},{2,3},{3,2},{4,5},{5,4},{6,7},{7,6},{8,9},{9,8},{10,11... | collective-permute-start | bytes 688136 | tf_op jit(solution)/shard_map/ppermute | solution.py:44
  319.0 8.4 %collective-permute-start.23 = (bf16[256,128]{1,0:T(8,128)(2,1)S(1)}, bf16[256,128]{1,0:T(8,128)(2,1)S(1)}, u32[]{:S(2)}, u32[]{:S(2)}) collective-permute-start(bf16[256,128]{1,0:T(8,128)(2,1)S(1)} %get-tuple-element.189), channel_id=1, source_target_pairs={{6,0},{7,1},{14,8},{15,9},{22,16},{23,17},{30,24},{31,25}} | collective-permute-start | bytes 196616 | tf_op jit(solution)/shard_map/ppermute | solution.py:346
  320.3 9.7 %collective-permute-start.22 = (bf16[256,128]{1,0:T(8,128)(2,1)S(1)}, bf16[256,128]{1,0:T(8,128)(2,1)S(1)}, u32[]{:S(2)}, u32[]{:S(2)}) collective-permute-start(bf16[256,128]{1,0:T(8,128)(2,1)S(1)} %get-tuple-element.190), channel_id=1, source_target_pairs={{4,0},{6,2},{5,1},{7,3},{12,8},{14,10},{13,9},{15,11},{20,16},{22,... | collective-permute-start | bytes 196616 | tf_op jit(solution)/shard_map/ppermute | solution.py:346
  321.6 8.4 %collective-permute-start.21 = (bf16[256,128]{1,0:T(8,128)(2,1)S(1)}, bf16[256,128]{1,0:T(8,128)(2,1)S(1)}, u32[]{:S(2)}, u32[]{:S(2)}) collective-permute-start(bf16[256,128]{1,0:T(8,128)(2,1)S(1)} %get-tuple-element.188), channel_id=1, source_target_pairs={{2,0},{4,2},{6,4},{3,1},{5,3},{7,5},{10,8},{12,10},{14,12},{11,9},... | collective-permute-start | bytes 196616 | tf_op jit(solution)/shard_map/ppermute | solution.py:346
  324.6 6.0 %copy-start.11 = (f32[256,512]{1,0:T(8,128)S(1)}, f32[256,512]{1,0:T(8,128)}, u32[]{:S(2)}) copy-start(f32[256,512]{1,0:T(8,128)} %copy-done.10) | copy-start | bytes 1572868
  324.6 6.0 %copy-start.13 = (f32[256,512]{1,0:T(8,128)S(1)}, f32[256,512]{1,0:T(8,128)}, u32[]{:S(2)}) copy-start(f32[256,512]{1,0:T(8,128)} %copy-done.12) | copy-start | bytes 1572868
  327.4 75.1 %collective-permute-start.40 = (bf16[2,3,224,608]{3,2,1,0:T(8,128)(2,1)}, bf16[2,3,224,608]{3,2,1,0:T(8,128)(2,1)}, u32[]{:S(2)}, u32[]{:S(2)}) collective-permute-start(bf16[2,3,224,608]{3,2,1,0:T(8,128)(2,1)} %pad_maximum_fusion.4), channel_id=1, source_target_pairs={{0,16},{1,9},{8,24},{9,1},{16,0},{17,25},{24,8},{25,17},{2,18},{3,... | collective-permute-start | bytes 4902920 | tf_op jit(solution)/shard_map/ppermute | solution.py:53
  333.6 6.9 %collective-permute-start.29 = (bf16[2,256,144]{1,2,0:T(8,128)(2,1)S(1)}, bf16[2,256,144]{1,2,0:T(8,128)(2,1)S(1)}, u32[]{:S(2)}, u32[]{:S(2)}) collective-permute-start(bf16[2,256,144]{1,2,0:T(8,128)(2,1)S(1)} %slice.460), channel_id=1, source_target_pairs={{0,8},{1,17},{8,0},{9,25},{16,24},{17,1},{24,16},{25,9},{2,10},{3,... | collective-permute-start | bytes 442376 | tf_op jit(solution)/shard_map/ppermute | solution.py:53
  335.2 5.9 %copy-start.15 = (bf16[896,576]{1,0:T(8,128)(2,1)S(1)}, bf16[896,576]{1,0:T(8,128)(2,1)}, u32[]{:S(2)}) copy-start(bf16[896,576]{1,0:T(8,128)(2,1)} %copy-done.14) | copy-start | bytes 3096580
  335.2 5.9 %copy-start.37 = (bf16[256,512]{1,0:T(8,128)(2,1)S(1)}, bf16[256,512]{1,0:T(8,128)(2,1)}, u32[]{:S(2)}) copy-start(bf16[256,512]{1,0:T(8,128)(2,1)} %copy-done.36) | copy-start | bytes 786436
  335.4 22.4 %copy-start.32 = (bf16[1,256,896]{2,1,0:T(8,128)(2,1)S(1)}, bf16[1,256,896]{2,1,0:T(8,128)(2,1)}, u32[]{:S(2)}) copy-start(bf16[1,256,896]{2,1,0:T(8,128)(2,1)} %copy-done.31) | copy-start | bytes 1376260
  336.2 25.4 %collective-permute-start.25 = (bf16[2,896,112]{1,2,0:T(8,128)(2,1)}, bf16[2,896,112]{1,2,0:T(8,128)(2,1)}, u32[]{:S(2)}, u32[]{:S(2)}) collective-permute-start(bf16[2,896,112]{1,2,0:T(8,128)(2,1)} %slice.457), channel_id=1, source_target_pairs={{0,8},{1,17},{8,0},{9,25},{16,24},{17,1},{24,16},{25,9},{2,10},{3,... | collective-permute-start | bytes 1204232 | tf_op jit(solution)/shard_map/ppermute | solution.py:53
  340.5 16.6 %copy-start.44 = (bf16[1,256,144]{1,2,0:T(8,128)(2,1)}, bf16[1,256,144]{1,2,0:T(8,128)(2,1)S(1)}, u32[]{:S(2)}) copy-start(bf16[1,256,144]{1,2,0:T(8,128)(2,1)S(1)} %get-tuple-element.191) | copy-start | bytes 221188
  340.5 16.5 %collective-permute-start.30 = (bf16[2,256,144]{1,2,0:T(8,128)(2,1)S(1)}, bf16[2,256,144]{1,2,0:T(8,128)(2,1)S(1)}, u32[]{:S(2)}, u32[]{:S(2)}) collective-permute-start(bf16[2,256,144]{1,2,0:T(8,128)(2,1)S(1)} %pad_maximum_fusion.23), channel_id=1, source_target_pairs={{0,16},{1,9},{8,24},{9,1},{16,0},{17,25},{24,8},{25,17},{2,18},{3,... | collective-permute-start | bytes 442376 | tf_op jit(solution)/shard_map/ppermute | solution.py:53
  341.7 22.3 %collective-permute-start.24 = (bf16[256,896]{1,0:T(8,128)(2,1)S(1)}, bf16[256,896]{1,0:T(8,128)(2,1)}, u32[]{:S(2)}, u32[]{:S(2)}) collective-permute-start(bf16[256,896]{1,0:T(8,128)(2,1)S(1)} %convolution_convert_fusion.5), channel_id=1, source_target_pairs={{0,1},{1,0},{2,3},{3,2},{4,5},{5,4},{6,7},{7,6},{8,9},{9,8},{10,11... | collective-permute-start | bytes 1376264 | tf_op jit(solution)/shard_map/ppermute | solution.py:44
  363.6 7.7 %copy-start.33 = (bf16[896,144]{1,0:T(8,128)(2,1)S(1)}, bf16[896,144]{1,0:T(8,128)(2,1)}, u32[]{:S(2)}) copy-start(bf16[896,144]{1,0:T(8,128)(2,1)} %copy.119) | copy-start | bytes 774148
  363.6 5.8 %collective-permute-start.26 = (bf16[896,112]{0,1:T(8,128)(2,1)S(1)}, bf16[896,112]{0,1:T(8,128)(2,1)S(1)}, u32[]{:S(2)}, u32[]{:S(2)}) collective-permute-start(bf16[896,112]{0,1:T(8,128)(2,1)S(1)} %fusion.60), channel_id=1, source_target_pairs={{0,16},{1,9},{8,24},{9,1},{16,0},{17,25},{24,8},{25,17},{2,18},{3,... | collective-permute-start | bytes 602120 | tf_op jit(solution)/shard_map/ppermute | solution.py:53
  372.4 18.7 %copy-start.17 = (bf16[256,896]{1,0:T(8,128)(2,1)S(1)}, bf16[256,896]{1,0:T(8,128)(2,1)}, u32[]{:S(2)}) copy-start(bf16[256,896]{1,0:T(8,128)(2,1)} %copy-done.16) | copy-start | bytes 1376260
  372.5 6.7 %collective-permute-start.33 = (bf16[240,256]{1,0:T(8,128)(2,1)S(1)}, bf16[240,256]{1,0:T(8,128)(2,1)S(1)}, u32[]{:S(2)}, u32[]{:S(2)}) collective-permute-start(bf16[240,256]{1,0:T(8,128)(2,1)S(1)} %get-tuple-element.174), channel_id=1, source_target_pairs={{0,6},{2,0},{4,2},{6,4},{1,7},{3,1},{5,3},{7,5},{8,14},{10,8},{12,... | collective-permute-start | bytes 368648 | tf_op jit(solution)/shard_map/ppermute | solution.py:308
  376.6 8.2 %collective-permute-start.32 = (bf16[240,256]{1,0:T(8,128)(2,1)S(1)}, bf16[240,256]{1,0:T(8,128)(2,1)S(1)}, u32[]{:S(2)}, u32[]{:S(2)}) collective-permute-start(bf16[240,256]{1,0:T(8,128)(2,1)S(1)} %get-tuple-element.175), channel_id=1, source_target_pairs={{0,4},{2,6},{4,0},{6,2},{1,5},{3,7},{5,1},{7,3},{8,12},{10,14},{12... | collective-permute-start | bytes 368648 | tf_op jit(solution)/shard_map/ppermute | solution.py:308
  376.6 8.1 %collective-permute-start.31 = (bf16[240,256]{1,0:T(8,128)(2,1)S(1)}, bf16[240,256]{1,0:T(8,128)(2,1)S(1)}, u32[]{:S(2)}, u32[]{:S(2)}) collective-permute-start(bf16[240,256]{1,0:T(8,128)(2,1)S(1)} %get-tuple-element.173), channel_id=1, source_target_pairs={{0,2},{2,4},{4,6},{6,0},{1,3},{3,5},{5,7},{7,1},{8,10},{10,12},{12... | collective-permute-start | bytes 368648 | tf_op jit(solution)/shard_map/ppermute | solution.py:308
  384.9 4.9 %collective-permute-start.34 = (bf16[240,256]{1,0:T(8,128)(2,1)S(1)}, bf16[240,256]{1,0:T(8,128)(2,1)S(1)}, u32[]{:S(2)}, u32[]{:S(2)}) collective-permute-start(bf16[240,256]{1,0:T(8,128)(2,1)S(1)} %get-tuple-element.194), channel_id=1, source_target_pairs={{0,8},{1,17},{8,0},{9,25},{16,24},{17,1},{24,16},{25,9},{2,10},{3,... | collective-permute-start | bytes 368648 | tf_op jit(solution)/shard_map/ppermute | solution.py:53
  389.9 6.3 %collective-permute-start.35 = (bf16[2,240,256]{2,1,0:T(8,128)(2,1)S(1)}, bf16[2,240,256]{2,1,0:T(8,128)(2,1)S(1)}, u32[]{:S(2)}, u32[]{:S(2)}) collective-permute-start(bf16[2,240,256]{2,1,0:T(8,128)(2,1)S(1)} %pad_maximum_fusion.21), channel_id=1, source_target_pairs={{0,16},{1,9},{8,24},{9,1},{16,0},{17,25},{24,8},{25,17},{2,18},{3,... | collective-permute-start | bytes 737288 | tf_op jit(solution)/shard_map/ppermute | solution.py:53
  (35 other events, 78.2 us)
